TPU v7x, 32 devices: a whole 2x2x4 slice. The times are simulated.
32 devices in a mesh: expert: 8 (over z, y), fsdp: 4 (over x, core).
Axes of the slice: x: 2, y: 2, z: 4, core: 2. Of those that a mesh axis runs over, the one named last changes fastest.
Arguments:
- feats: bfloat16 [128, 128, 1536], P('expert', None, 'fsdp'), may hold values from -6 to 6
- cotan: bfloat16 [128, 128, 1536], P('expert', None, 'fsdp'), may hold values from -6 to 6
- lang: int32 [128], P('expert'), may hold values from 0 to 7, as said below
- w_out: bfloat16 [8, 1536, 1536], P('expert', 'fsdp'), may hold values from -0.15625 to 0.15625
- gain: bfloat16 [8, 1536], P('expert', 'fsdp'), may hold values from 0.099609375 to 1.8984375
- kernel: bfloat16 [8, 31, 1536], P('expert', None, 'fsdp'), may hold values from -1 to 1
Outputs:
- feat_grad: bfloat16 [128, 128, 1536], P('expert', None, 'fsdp')
- w_grad: bfloat16 [8, 1536, 1536], P('expert', 'fsdp')
- gain_grad: float32 [8, 1536], P('expert', 'fsdp')
- kernel_grad: float32 [8, 31, 1536], P('expert', None, 'fsdp')
Inputs may be any that keep to these rules, and one draw needn't show every extreme that they name: `lang`: each index of the expert axis holds either none or exactly 4 segments of a language, and each language has exactly 16 segments in all.
All inputs are finite; a program needn't handle non-finite values.
Results may differ from a plain program's by a relative error of at most 0.005.
Values may be sent and summed in bfloat16 or wider, within the bound.
No kernel may reach another device: no remote copies, remote signals or barrier semaphores. Data moves between devices by JAX's collectives and lax.ppermute only.
A program may use at most 128 MiB of HBM per device.

v0:
```python
import jax
import jax.numpy as jnp
from jax import lax
from jax.sharding import PartitionSpec as P


def normalize(values, feature_total):
    value_sum = lax.psum(jnp.sum(values, axis=-1), "fsdp")
    centre = values - (value_sum / feature_total)[..., None]
    square_sum = lax.psum(jnp.sum(centre * centre, axis=-1), "fsdp")
    row_var = square_sum / feature_total
    inv_std = lax.rsqrt(row_var + 1e-05)[..., None]
    return (centre * inv_std, inv_std)


def forward_part(inputs, norm_gain, conv_taps, feature_total):
    normed, inv_std = normalize(inputs.astype(jnp.float32), feature_total)
    scaled = normed * norm_gain
    tap_count = conv_taps.shape[0]
    half_width = tap_count // 2
    frames = inputs.shape[1]
    padded = jnp.pad(scaled, ((0, 0), (half_width, half_width), (0, 0)))
    conv_out = jnp.zeros_like(scaled)
    for offset in range(tap_count):
        conv_out = conv_out + conv_taps[offset] * padded[:, offset : offset + frames]
    gate_sig = jax.nn.sigmoid(conv_out)
    hidden = (conv_out * gate_sig).astype(jnp.bfloat16)
    return (normed, inv_std, padded, conv_out, gate_sig, hidden)


def back_split(
    hid_grad,
    grads_in,
    normed,
    inv_std,
    padded,
    conv_out,
    gate_sig,
    norm_gain,
    conv_taps,
    feature_total,
):
    tap_count = conv_taps.shape[0]
    half_width = tap_count // 2
    frames = normed.shape[1]
    conv_grad = hid_grad * gate_sig * (1.0 + conv_out * (1.0 - gate_sig))
    grad_padded = jnp.pad(conv_grad, ((0, 0), (half_width, half_width), (0, 0)))
    scaled_grad = jnp.zeros_like(conv_grad)
    tap_grads = []
    for offset in range(tap_count):
        first_row = 2 * half_width - offset
        scaled_grad = (
            scaled_grad + conv_taps[offset] * grad_padded[:, first_row : first_row + frames]
        )
        tap_grads.append(jnp.sum(conv_grad * padded[:, offset : offset + frames], axis=(0, 1)))
    gain_grad = jnp.sum(scaled_grad * normed, axis=(0, 1))
    norm_grad = scaled_grad * norm_gain
    grad_total, cross_total = lax.psum(
        (jnp.sum(norm_grad, axis=-1), jnp.sum(norm_grad * normed, axis=-1)), "fsdp"
    )
    branch = inv_std * (
        norm_grad
        - (grad_total / feature_total)[..., None]
        - normed * (cross_total / feature_total)[..., None]
    )
    input_grad = (grads_in.astype(jnp.float32) + branch).astype(jnp.bfloat16)
    return (input_grad, gain_grad, jnp.stack(tap_grads))


def arrival_map(recv_occupied, seg_count):
    flat_occupied = recv_occupied.reshape(-1)
    order_pos = jnp.cumsum(flat_occupied) - 1
    position = jnp.arange(seg_count, dtype=jnp.int32)
    return ((order_pos[None, :] == position[:, None]) & (flat_occupied[None, :] > 0)).astype(
        jnp.bfloat16
    )


def compact_rows(compact_map, received, row_shape):
    flat = received.reshape(compact_map.shape[1], -1)
    return (
        jnp.dot(compact_map, flat, preferred_element_type=jnp.float32)
        .astype(jnp.bfloat16)
        .reshape(row_shape)
    )


def per_device(feats, cotan, lang, w_out, gain, kernel):
    seg_count, frames, part_width = feats.shape
    owners = lax.axis_size("expert")
    feature_total = part_width * lax.axis_size("fsdp")
    capacity = max(1, 2 * seg_count // owners)
    slot_count = owners * capacity
    position = jnp.arange(seg_count, dtype=jnp.int32)
    earlier_same = (lang[:, None] == lang[None, :]) & (position[:, None] < position[None, :])
    slot_rank = jnp.sum(earlier_same.astype(jnp.int32), axis=0)
    slot_of = lang * capacity + slot_rank
    routing = jnp.arange(slot_count, dtype=jnp.int32)[:, None] == slot_of[None, :]
    routing_b = routing.astype(jnp.bfloat16)
    send_x = (
        jnp.dot(routing_b, feats.reshape(seg_count, -1), preferred_element_type=jnp.float32)
        .astype(jnp.bfloat16)
        .reshape(owners, capacity, -1)
    )
    send_dy = (
        jnp.dot(routing_b, cotan.reshape(seg_count, -1), preferred_element_type=jnp.float32)
        .astype(jnp.bfloat16)
        .reshape(owners, capacity, -1)
    )
    occupied = jnp.sum(routing.astype(jnp.int32), axis=1).reshape(owners, capacity)
    norm_gain = gain[0].astype(jnp.float32)
    conv_taps = kernel[0].astype(jnp.float32)
    row_shape = (seg_count, frames, part_width)
    recv_x, recv_dy, recv_occupied = (
        lax.all_to_all(send_x, "expert", split_axis=0, concat_axis=0, tiled=True),
        lax.all_to_all(send_dy, "expert", split_axis=0, concat_axis=0, tiled=True),
        lax.all_to_all(occupied, "expert", split_axis=0, concat_axis=0, tiled=True),
    )
    compact_map = arrival_map(recv_occupied, seg_count)
    own_x = compact_rows(compact_map, recv_x, row_shape)
    forward = forward_part(own_x, norm_gain, conv_taps, feature_total)
    own_dy = compact_rows(compact_map, recv_dy, row_shape)
    normed, inv_std, padded, conv_out, gate_sig, hidden = forward
    grad_scale = float(seg_count * frames) ** (-0.5)
    hidden_rows = hidden.reshape(-1, part_width)
    w_rows = w_out[0]
    shard_part = lax.all_gather(own_dy.reshape(-1, part_width), "fsdp", axis=1, tiled=True)
    hid_sum = jnp.dot(shard_part, w_rows.T, preferred_element_type=jnp.float32)
    w_block = jnp.dot(hidden_rows.T, shard_part, preferred_element_type=jnp.float32) * grad_scale
    w_sum = w_block
    hid_sum, w_sum = (hid_sum, w_sum)
    hid_grad = hid_sum.reshape(row_shape)
    input_grad, gain_grad, tap_grad = back_split(
        hid_grad,
        own_dy,
        normed,
        inv_std,
        padded,
        conv_out,
        gate_sig,
        norm_gain,
        conv_taps,
        feature_total,
    )
    back_slots = jnp.dot(
        compact_map.T, input_grad.reshape(seg_count, -1), preferred_element_type=jnp.float32
    ).astype(jnp.bfloat16)
    home_slots = lax.all_to_all(
        back_slots.reshape(owners, capacity, -1), "expert", split_axis=0, concat_axis=0, tiled=True
    )
    feat_grad = (
        jnp.dot(routing_b.T, home_slots.reshape(slot_count, -1), preferred_element_type=jnp.float32)
        .astype(jnp.bfloat16)
        .reshape(feats.shape)
    )
    return (
        feat_grad,
        w_sum.astype(jnp.bfloat16)[None],
        (gain_grad * grad_scale)[None],
        (tap_grad * grad_scale)[None],
    )


def solution(mesh):
    in_specs = (
        P("expert", None, "fsdp"),
        P("expert", None, "fsdp"),
        P("expert"),
        P("expert", "fsdp", None),
        P("expert", "fsdp"),
        P("expert", None, "fsdp"),
    )
    out_specs = (
        P("expert", None, "fsdp"),
        P("expert", "fsdp", None),
        P("expert", "fsdp"),
        P("expert", None, "fsdp"),
    )
    return jax.shard_map(
        per_device, mesh=mesh, in_specs=in_specs, out_specs=out_specs, check_vma=False
    )
```

profile of v0, /device:TPU:0, one launch (start us, length us, event | category | flops | bytes accessed | tf_op | source)
XLA Modules:
  0.0 410.2 jit_solution(9826892604606808070)
XLA Ops:
  9.5 7.3 %all-to-all-start = ((s32[8,1,4]{2,1,0:T(1,128)}), s32[8,1,4]{2,1,0:T(1,128)S(1)}, u32[]{:S(2)}, u32[]{:S(2)}) async-start(s32[8,1,4]{2,1,0:T(1,128)} %bitcast), calls=%async_computation | async-start | bytes 8192 | tf_op jit(solution)/shard_map/all_to_all | solution.py:117
  16.7 2.3 copy.16
  19.1 2.7 convolution_convert_fusion.2
  21.8 4.7 %reshape.649 = bf16[8,4,49152]{2,1,0:T(4,128)(2,1)} reshape(bf16[32,49152]{1,0:T(8,128)(2,1)} %convolution_convert_fusion.2) | data formatting | bytes 6291456 | tf_op jit(solution)/shard_map/reshape | solution.py:108
  26.5 6.1 %all-to-all-start.1 = ((bf16[8,4,49152]{2,1,0:T(4,128)(2,1)}), bf16[8,4,49152]{2,1,0:T(4,128)(2,1)}, u32[]{:S(2)}, u32[]{:S(2)}) async-start(bf16[8,4,49152]{2,1,0:T(4,128)(2,1)} %reshape.649), calls=%async_computation.1 | async-start | bytes 6291456 | tf_op jit(solution)/shard_map/all_to_all | solution.py:116
  33.6 2.7 convolution_convert_fusion.1
  36.3 4.7 %reshape.652 = bf16[8,4,49152]{2,1,0:T(4,128)(2,1)} reshape(bf16[32,49152]{1,0:T(8,128)(2,1)} %convolution_convert_fusion.1) | data formatting | bytes 6291456 | tf_op jit(solution)/shard_map/reshape | solution.py:103
  42.6 60.3 %all-to-all-done.1 = bf16[8,4,49152]{2,1,0:T(4,128)(2,1)} async-done(((bf16[8,4,49152]{2,1,0:T(4,128)(2,1)}), bf16[8,4,49152]{2,1,0:T(4,128)(2,1)}, u32[]{:S(2)}, u32[]{:S(2)}) %all-to-all-start.1) | async-done | bytes 3145760 | tf_op jit(solution)/shard_map/all_to_all | solution.py:116
  102.9 4.4 %all-to-all-start.2 = ((bf16[8,4,49152]{2,1,0:T(4,128)(2,1)}), bf16[8,4,49152]{2,1,0:T(4,128)(2,1)}, u32[]{:S(2)}, u32[]{:S(2)}) async-start(bf16[8,4,49152]{2,1,0:T(4,128)(2,1)} %reshape.652), calls=%async_computation.2 | async-start | bytes 6291456 | tf_op jit(solution)/shard_map/all_to_all | solution.py:115
  107.4 4.6 %reshape.650 = bf16[32,49152]{1,0:T(8,128)(2,1)} reshape(bf16[8,4,49152]{2,1,0:T(4,128)(2,1)} %all-to-all-done.1) | data formatting | bytes 6291456 | tf_op jit(solution)/shard_map/reshape | solution.py:80
  112.0 2.4 convolution_convert_fusion.5
  116.3 61.2 %all-to-all-done.2 = bf16[8,4,49152]{2,1,0:T(4,128)(2,1)} async-done(((bf16[8,4,49152]{2,1,0:T(4,128)(2,1)}), bf16[8,4,49152]{2,1,0:T(4,128)(2,1)}, u32[]{:S(2)}, u32[]{:S(2)}) %all-to-all-start.2) | async-done | bytes 3145760 | tf_op jit(solution)/shard_map/all_to_all | solution.py:115
  177.6 4.6 %reshape.653 = bf16[32,49152]{1,0:T(8,128)(2,1)} reshape(bf16[8,4,49152]{2,1,0:T(4,128)(2,1)} %all-to-all-done.2) | data formatting | bytes 6291456 | tf_op jit(solution)/shard_map/reshape | solution.py:80
  182.2 2.4 fusion
  185.2 2.3 copy.17
  188.3 5.8 %psum.28 = f32[16,128]{1,0:T(8,128)S(1)} all-reduce(f32[16,128]{1,0:T(8,128)S(1)} %bitcast_reduce_fusion), channel_id=1, replica_groups=mesh['expert'=8,'fsdp'=4] {'fsdp'}, use_global_device_ids=true, to_apply=%region_4.5 | all-reduce | flops 2048 | bytes 16384 | tf_op jit(solution)/shard_map/psum | solution.py:8
  194.1 2.5 multiply_reduce_fusion.33
  196.6 6.9 %psum.29 = f32[16,128]{1,0:T(8,128)S(1)} all-reduce(f32[16,128]{1,0:T(8,128)S(1)} %multiply_reduce_fusion.33), channel_id=1, replica_groups=mesh['expert'=8,'fsdp'=4] {'fsdp'}, use_global_device_ids=true, to_apply=%region_6.7 | all-reduce | flops 2048 | bytes 16384 | tf_op jit(solution)/shard_map/psum | solution.py:10
  203.5 2.3 fusion.65
  207.5 13.3 %multiply_convert_fusion = (bf16[16,128,384]{2,1,0:T(8,128)(2,1)S(1)}, f32[16,128,384]{2,1,0:T(8,128)}) fusion(f32[384]{0:T(512)S(1)} %get-tuple-element.39, f32[384]{0:T(512)S(1)} %get-tuple-element.40, f32[384]{0:T(512)S(1)} %get-tuple-element.41, f32[384]{0:T(512)S(1)} %get-tuple-element.42, f32[384]{0:T(512)S(1)} %get-tuple-element.43, ...), kind=kLoop, calls=%fused_computation.163 | loop fusion | flops 51904512 | bytes 7911936 | tf_op jit(solution)/shard_map/convert_element_type | solution.py:27
  220.8 27.2 %multiply_reduce_fusion.18 = (f32[384]{0:T(512)S(1)}, f32[384]{0:T(512)S(1)}, f32[384]{0:T(512)S(1)}, f32[384]{0:T(512)S(1)}, f32[384]{0:T(512)S(1)}, /*index=5*...) fusion(f32[16,128,384]{2,1,0:T(8,128)} %copy-done.3, ...), kind=kOutput, calls=%fused_computation.149 | convolution fusion | flops 2442651136 | bytes 16928256 | tf_op jit(solution)/shard_map/dot_general | solution.py:128
  248.0 49.5 %multiply_reduce_fusion.31 = (f32[384]{0:T(512)S(1)}, f32[16,128]{1,0:T(8,128)S(1)}, f32[16,128]{1,0:T(8,128)S(1)}, f32[16,128,384]{2,1,0:T(8,128)}) fusion(f32[2,8,128,384]{3,2,1,0:T(8,128)} %copy-done.2, f32[16,128]{1,0:T(8,128)S(1)} %add_rsqrt_fusion, f32[16,128]{1,0:T(8,128)S(1)} %broadcast_multiply_fusion.3, f32[384]{0:T(512)S(1)} %convert_reduce_fusion.2, ...), kind=kLoop, calls=%fused_computation.162 | loop fusion | flops 54259328 | bytes 9520640 | tf_op jit(solution)/shard_map/reduce_sum | solution.py:56
  297.5 10.2 %all-reduce.2 = (f32[16,128]{1,0:T(8,128)S(1)}, f32[16,128]{1,0:T(8,128)S(1)}) all-reduce(f32[16,128]{1,0:T(8,128)S(1)} %get-tuple-element.5, f32[16,128]{1,0:T(8,128)S(1)} %get-tuple-element.37), channel_id=1, replica_groups=mesh['expert'=8,'fsdp'=4] {'fsdp'}, use_global_device_ids=true, to_apply=%region_10.11 | all-reduce | flops 4096 | bytes 32768 | tf_op jit(solution)/shard_map/psum | solution.py:58
  307.8 4.4 %fusion.61 = bf16[16,128,384]{2,1,0:T(8,128)(2,1)S(1)} fusion(f32[2,8,128,384]{3,2,1,0:T(8,128)} %copy.17, f32[16,128,384]{2,1,0:T(8,128)} %get-tuple-element.73, f32[2,8,128,384]{3,2,1,0:T(8,128)} %copy-done.2, f32[16,128]{1,0:T(8,128)S(1)} %get-tuple-element.75, f32[16,128]{1,0:T(8,128)S(1)} %get-tuple-element.76, f32[384]{0:T(512)S(1)} %convert_reduce_fusion.2, ...), kind=kLoop, calls=%fused_computation.130 | loop fusion | flops 7077888 | bytes 11044352 | tf_op jit(solution)/shard_map/convert_element_type | solution.py:66
  313.1 2.7 convolution_convert_fusion
  315.8 4.7 %reshape.655 = bf16[8,4,49152]{2,1,0:T(4,128)(2,1)} reshape(bf16[32,49152]{1,0:T(8,128)(2,1)} %convolution_convert_fusion) | data formatting | bytes 6291456 | tf_op jit(solution)/shard_map/reshape | solution.py:149
  320.5 4.7 %all-to-all-start.3 = ((bf16[8,4,49152]{2,1,0:T(4,128)(2,1)}), bf16[8,4,49152]{2,1,0:T(4,128)(2,1)}, u32[]{:S(2)}, u32[]{:S(2)}) async-start(bf16[8,4,49152]{2,1,0:T(4,128)(2,1)} %reshape.655), calls=%async_computation.3 | async-start | bytes 6291456 | tf_op jit(solution)/shard_map/all_to_all | solution.py:148
  326.0 30.9 %multiply_reduce_fusion = (f32[384]{0:T(512)S(1)}, f32[384]{0:T(512)S(1)}, f32[384]{0:T(512)S(1)}, f32[384]{0:T(512)S(1)}, f32[384]{0:T(512)S(1)}, /*index=5*/f3...) fusion(f32[16,128,384]{2,1,0:T(8,128)} %get-tuple-element.74, ...), kind=kLoop, calls=%fused_computation.131 | loop fusion | flops 28304640 | bytes 6319104 | tf_op jit(solution)/shard_map/reduce_sum | solution.py:55
  357.8 6.4 %fusion.64 = bf16[1,384,1536]{2,1,0:T(8,128)(2,1)} fusion(bf16[2048,384]{1,0:T(8,128)(2,1)S(1)} %bitcast.60, bf16[2048,1536]{1,0:T(8,128)(2,1)} %all-gather.2.cloned.1.call-done), kind=kOutput, calls=%fused_computation.173 | convolution fusion | flops 2417098752 | bytes 9043968 | tf_op jit(solution)/shard_map/dot_general | solution.py:129
  364.2 30.7 %all-to-all-done.3 = bf16[8,4,49152]{2,1,0:T(4,128)(2,1)} async-done(((bf16[8,4,49152]{2,1,0:T(4,128)(2,1)}), bf16[8,4,49152]{2,1,0:T(4,128)(2,1)}, u32[]{:S(2)}, u32[]{:S(2)}) %all-to-all-start.3) | async-done | bytes 3145760 | tf_op jit(solution)/shard_map/all_to_all | solution.py:148
  394.9 4.6 %reshape.656 = bf16[32,49152]{1,0:T(8,128)(2,1)} reshape(bf16[8,4,49152]{2,1,0:T(4,128)(2,1)} %all-to-all-done.3) | data formatting | bytes 6291456 | tf_op jit(solution)/shard_map/reshape | solution.py:152
  399.5 2.5 convolution_convert_fusion.3
  (76 shorter events, 13.6 us)
Async XLA Ops:
  7.2 213.7 %copy-start = (bf16[1,384,1536]{2,1,0:T(8,128)(2,1)S(1)}, bf16[1,384,1536]{2,1,0:T(8,128)(2,1)}, u32[]{:S(2)}) copy-start(bf16[1,384,1536]{2,1,0:T(8,128)(2,1)} %param.9) | copy-start | bytes 3538948
  9.5 17.1 %all-to-all-start = ((s32[8,1,4]{2,1,0:T(1,128)}), s32[8,1,4]{2,1,0:T(1,128)S(1)}, u32[]{:S(2)}, u32[]{:S(2)}) async-start(s32[8,1,4]{2,1,0:T(1,128)} %bitcast), calls=%async_computation | async-start | bytes 8192 | tf_op jit(solution)/shard_map/all_to_all | solution.py:117
  26.5 6.1 %copy-start.4 = (bf16[16,128,384]{2,1,0:T(8,128)(2,1)S(1)}, bf16[16,128,384]{2,1,0:T(8,128)(2,1)}, u32[]{:S(2)}) copy-start(bf16[16,128,384]{2,1,0:T(8,128)(2,1)} %param.6) | copy-start | bytes 4718596
  26.5 76.4 %all-to-all-start.1 = ((bf16[8,4,49152]{2,1,0:T(4,128)(2,1)}), bf16[8,4,49152]{2,1,0:T(4,128)(2,1)}, u32[]{:S(2)}, u32[]{:S(2)}) async-start(bf16[8,4,49152]{2,1,0:T(4,128)(2,1)} %reshape.649), calls=%async_computation.1 | async-start | bytes 6291456 | tf_op jit(solution)/shard_map/all_to_all | solution.py:116
  102.9 74.6 %all-to-all-start.2 = ((bf16[8,4,49152]{2,1,0:T(4,128)(2,1)}), bf16[8,4,49152]{2,1,0:T(4,128)(2,1)}, u32[]{:S(2)}, u32[]{:S(2)}) async-start(bf16[8,4,49152]{2,1,0:T(4,128)(2,1)} %reshape.652), calls=%async_computation.2 | async-start | bytes 6291456 | tf_op jit(solution)/shard_map/all_to_all | solution.py:115
  107.4 113.5 %all-gather.2.cloned.1.call-start = ((), (), s32[]{:S(2)}) async-start(), calls=%async_computation.4 | async-start | bytes 7864320 | tf_op jit(solution)/shard_map/all_gather | solution.py:127
  114.4 1.7 copy-start.5
  114.4 1.7 copy-start.6
  185.2 2.7 copy-start.2
  205.8 1.7 copy-start.3
  320.5 74.3 %all-to-all-start.3 = ((bf16[8,4,49152]{2,1,0:T(4,128)(2,1)}), bf16[8,4,49152]{2,1,0:T(4,128)(2,1)}, u32[]{:S(2)}, u32[]{:S(2)}) async-start(bf16[8,4,49152]{2,1,0:T(4,128)(2,1)} %reshape.655), calls=%async_computation.3 | async-start | bytes 6291456 | tf_op jit(solution)/shard_map/all_to_all | solution.py:148
  394.9 8.5 %copy-start.1 = (bf16[1,384,1536]{2,1,0:T(8,128)(2,1)S(1)}, bf16[1,384,1536]{2,1,0:T(8,128)(2,1)}, u32[]{:S(2)}) copy-start(bf16[1,384,1536]{2,1,0:T(8,128)(2,1)} %param.9) | copy-start | bytes 3538948
Sparse Core Ops, SparseCore 0:
  116.2 47.5 all-gather.1
where the time goes:
time: 411 us; the launch traced here: 410 us
  waiting for transfers between devices  152 us (37%)
  other arithmetic  106 us (26%)
  matrix products  49.2 us (12%)
  local copies, waits for them, and re-layouts  42.6 us (10%)
  blocking collectives  22.9 us (6%)
  starting transfers between devices  22.6 us (5%)
  between operations  14.3 us (3%)
    all_to_all x1, waiting for transfers between devices, per_device(): lax.all_to_all(send_x, 'expert', split_axis=0, concat_axis=0, tiled=True)  61.2 us
    all_to_all x1, waiting for transfers between devices, per_device(): lax.all_to_all(send_dy, 'expert', split_axis=0, concat_axis=0, tiled=True)  60.3 us
    reduce_sum x1, other arithmetic, back_split(): gain_grad = jnp.sum(scaled_grad * normed, axis=(0, 1))  49.5 us
    reduce_sum x1, other arithmetic, back_split(): jnp.sum(conv_grad * padded[:, offset:offset + frames], axis=(0, 1))  30.9 us
    all_to_all x1, waiting for transfers between devices, per_device(): lax.all_to_all(back_slots.reshape(owners, capacity, -1), 'expert', split_...  30.7 us
    dot_general x1, matrix products, per_device(): hid_sum = jnp.dot(shard_part, w_rows.T, preferred_element_type=jnp.float32)  27.2 us
    convert_element_type x1, other arithmetic, forward_part(): hidden = (conv_out * gate_sig).astype(jnp.bfloat16)  13.3 us
    unnamed x50, local copies, waits for them, and re-layouts  10.9 us
  transfers between devices with their start and end apart: 5, of which 3 were waited for; matrix products, arithmetic and copies ran while one was open for 23% of the time, Pallas kernels for 0%

commit v1 on v0

--- a/solution.py
+++ b/solution.py
@@ -1,8 +1,18 @@
+import math
+
 import jax
 import jax.numpy as jnp
+import ml_dtypes
+import numpy as np
 from jax import lax
+from jax.experimental import pallas as pl
+from jax.experimental.pallas import tpu as pltpu
 from jax.sharding import PartitionSpec as P
 
+BF16 = jnp.bfloat16
+F32 = jnp.float32
+VMEM_BYTES = 60 * 1024 * 1024
+WEIGHT = {"front": 30, "frame_stats": 30, "tap_waves": 30, "w_grad": 30}
 
 def normalize(values, feature_total):
     value_sum = lax.psum(jnp.sum(values, axis=-1), "fsdp")
@@ -85,7 +95,7 @@
     )
 
 
-def per_device(feats, cotan, lang, w_out, gain, kernel):
+def routed_frames(feats, cotan, lang, w_out, gain, kernel):
     seg_count, frames, part_width = feats.shape
     owners = lax.axis_size("expert")
     feature_total = part_width * lax.axis_size("fsdp")
@@ -161,6 +171,716 @@
     )
 
 
+def split_const(matrix):
+    high = matrix.astype(ml_dtypes.bfloat16)
+    low = (matrix - high.astype(np.float64)).astype(ml_dtypes.bfloat16)
+    return np.concatenate([high, high, low], axis=1)
+
+
+def wave_tables(frames, taps):
+    half = taps // 2
+    period = -(-(frames + half) // 16) * 16
+    omega = 2 * np.pi * (np.arange(period // 2) + 0.5) / period
+    angle = omega[:, None] * np.arange(frames)
+    forward = np.concatenate([np.cos(angle), np.sin(angle)], axis=0)
+    lag_angle = omega[:, None] * (np.arange(taps) - half)
+    tap_wave = np.concatenate([np.cos(lag_angle), np.sin(lag_angle)], axis=0)
+    tap_wave = np.pad(tap_wave, ((0, 0), (0, 1)))
+    lag_wave = np.concatenate([np.cos(lag_angle), -np.sin(lag_angle)], axis=0).T * (2 / period)
+    lag_wave = np.pad(lag_wave, ((0, 1), (0, 0)))
+    tap_high = tap_wave.astype(ml_dtypes.bfloat16)
+    tap_low = (tap_wave - tap_high.astype(np.float64)).astype(ml_dtypes.bfloat16)
+    return (
+        split_const(forward),
+        split_const(forward.T * (2 / period)),
+        np.stack([tap_high, tap_low]),
+        split_const(lag_wave),
+        period,
+    )
+
+
+def wide_dot(const_terms, values):
+    high = values.astype(BF16)
+    low = (values - high.astype(F32)).astype(BF16)
+    stacked = jnp.concatenate([high, low, high], axis=0)
+    return jnp.dot(const_terms, stacked, preferred_element_type=F32)
+
+
+def down_lanes(row, width):
+    frames = row.shape[1]
+    square = jnp.broadcast_to(row, (frames, frames)).T
+    return jnp.concatenate([square] * (width // frames), axis=1)
+
+
+def across_lanes(first, second):
+    frames = first.shape[0]
+    lane = lax.broadcasted_iota(jnp.int32, (frames, frames), 1)
+    square = jnp.where(lane == 0, first, jnp.where(lane == 1, second, 0.0))
+    return square.T[0:8]
+
+
+def side_by_side(pieces):
+    return jnp.concatenate(pieces, axis=1) if len(pieces) > 1 else pieces[0]
+
+
+def row_stats(stat_refs, part_width):
+    total = part_width * len(stat_refs)
+    sums = [ref[0, 0:1, :] for ref in stat_refs]
+    squares = [ref[0, 1:2, :] for ref in stat_refs]
+    mean = sum(sums) / total
+    spread = sum(squares)
+    for part_sum in sums:
+        shift = part_sum / part_width - mean
+        spread = spread + part_width * (shift * shift)
+    return mean, lax.rsqrt(spread / total + 1e-05)
+
+
+def stats_kernel(x_ref, stat_out):
+    for one in range(x_ref.shape[0]):
+        values = x_ref[one].astype(F32)
+        part_width = values.shape[1]
+        part_sum = jnp.sum(values, axis=1, keepdims=True)
+        centre = values - part_sum / part_width
+        stat_out[one] = across_lanes(part_sum, jnp.sum(centre * centre, axis=1, keepdims=True))
+
+
+def tap_kernel(wave_ref, *refs):
+    tap_refs, out_ref = refs[:-1], refs[-1]
+    period, count = wave_ref.shape[1:]
+    at = 0
+    for tap_ref in tap_refs:
+        for one in range(tap_ref.shape[0]):
+            taps = tap_ref[one, :count]
+            out_ref[at, :period] = jnp.dot(
+                wave_ref[0], taps, preferred_element_type=F32
+            ) + jnp.dot(wave_ref[1], taps, preferred_element_type=F32)
+            gain = taps.astype(F32)[taps.shape[0] - 1 :]
+            out_ref[at, period:] = jnp.broadcast_to(gain, (8, gain.shape[1]))
+            at += 1
+
+
+def normed_of(x_ref, rows):
+    values = x_ref[0].astype(F32)
+    width = values.shape[1]
+    spread = down_lanes(rows[1:2], width)
+    return (values - down_lanes(rows[0:1], width)) * spread, spread
+
+
+def front_kernel(cap, parts, own_ref, *refs):
+    refs = list(refs)
+    x_refs = [refs.pop(0) for _ in range(cap)]
+    stat_refs = [[refs.pop(0) for _ in range(cap)] for _ in range(parts)]
+    tap_ref, fwd_ref, inv_ref, *hid_outs, conv_out, wave_out, row_out = refs
+    width = x_refs[0].shape[2]
+    period = wave_out.shape[1]
+    gain = tap_ref[0, period : period + 1]
+    scaled = []
+    for one in range(cap):
+        mean, inv_std = row_stats([ref[one] for ref in stat_refs], width)
+        row = lax.broadcasted_iota(jnp.int32, row_out.shape[1:], 0)
+        rows = jnp.where(row == 0, mean, jnp.where(row == 1, inv_std, 0.0))
+        row_out[one] = rows
+        scaled.append(normed_of(x_refs[one], rows)[0] * gain)
+    wave = wide_dot(fwd_ref[...], side_by_side(scaled))
+    count = wave.shape[0] // 2
+    a, b = wave[:count], wave[count:]
+    kc = side_by_side([tap_ref[0, :count]] * cap)
+    ks = side_by_side([tap_ref[0, count : 2 * count]] * cap)
+    conv = wide_dot(inv_ref[...], jnp.concatenate([a * kc + b * ks, b * kc - a * ks], axis=0))
+    hidden = (conv * jax.nn.sigmoid(conv)).astype(BF16)
+    frames = conv.shape[0]
+    for one in range(cap):
+        at = slice(one * width, (one + 1) * width)
+        conv_out[one] = conv[:, at]
+        wave_out[one] = wave[:, at]
+        first = one * width
+        for hid_out in hid_outs:
+            cut = hid_out.shape[2]
+            hid_out[0, one * frames : (one + 1) * frames] = hidden[:, first : first + cut]
+            first += cut
+
+
+def back_kernel(cap, own_ref, *refs):
+    x_refs = refs[:cap]
+    (
+        row_ref,
+        tap_ref,
+        fwd_ref,
+        inv_ref,
+        lag_ref,
+        own_grad_ref,
+        recv_ref,
+        conv_ref,
+        wave_ref,
+        grad_out,
+        sum_out,
+        small_out,
+    ) = refs[cap:]
+    segs = conv_ref.shape[0] * pl.num_programs(0)
+    period = wave_ref.shape[1]
+    mine = (own_ref[segs + pl.program_id(0) * cap] & 1) == (own_ref[2 * segs] & 1)
+    gain = tap_ref[0, period : period + 1]
+    frames, width = x_refs[0].shape[1:]
+    normed = [normed_of(x_refs[one], row_ref[one])[0] for one in range(cap)]
+    hid_grad = jnp.where(mine, own_grad_ref[0], recv_ref[0]).astype(F32)
+    hid_grad = side_by_side([hid_grad[one * frames : (one + 1) * frames] for one in range(cap)])
+    conv = side_by_side([conv_ref[one] for one in range(cap)])
+    gate = jax.nn.sigmoid(conv)
+    conv_grad = hid_grad * gate * (1.0 + conv * (1.0 - gate))
+    grad_wave = wide_dot(fwd_ref[...], conv_grad)
+    count = grad_wave.shape[0] // 2
+    ga, gb = grad_wave[:count], grad_wave[count:]
+    wave = side_by_side([wave_ref[one] for one in range(cap)])
+    a, b = wave[:count], wave[count:]
+    kc = side_by_side([tap_ref[0, :count]] * cap)
+    ks = side_by_side([tap_ref[0, count : 2 * count]] * cap)
+    cross = jnp.concatenate([ga * a + gb * b, gb * a - ga * b], axis=0)
+    cross = sum(cross[:, one * width : (one + 1) * width] for one in range(cap))
+    scaled_grad = wide_dot(
+        inv_ref[...], jnp.concatenate([ga * kc - gb * ks, ga * ks + gb * kc], axis=0)
+    )
+    gain_grad = None
+    for one in range(cap):
+        part = scaled_grad[:, one * width : (one + 1) * width]
+        product = part * normed[one]
+        gain_grad = product if gain_grad is None else gain_grad + product
+        norm_grad = part * gain
+        grad_out[one] = norm_grad
+        sum_out[one] = across_lanes(
+            jnp.sum(norm_grad, axis=1, keepdims=True),
+            jnp.sum(norm_grad * normed[one], axis=1, keepdims=True),
+        )
+    tap_rows = wide_dot(lag_ref[...], cross)
+    gain_row = jnp.sum(gain_grad, axis=0, keepdims=True)
+    row = lax.broadcasted_iota(jnp.int32, tap_rows.shape, 0)
+    small_out[0] = jnp.where(row == tap_rows.shape[0] - 1, gain_row, tap_rows)
+
+
+def final_kernel(cap, chunks, order_ref, *refs):
+    x_refs, dy_refs, grad_refs = refs[:cap], refs[cap : 2 * cap], refs[2 * cap : 2 * cap + chunks]
+    row_ref, *sum_refs, out_ref, out_buf, sems = refs[2 * cap + chunks :]
+    step, last = pl.program_id(0), pl.num_programs(0) - 1
+    parts, width = len(sum_refs), x_refs[0].shape[2]
+    slot = step % 2
+
+    def put(slot, step, one):
+        return pltpu.make_async_copy(
+            out_buf.at[slot, one], out_ref.at[order_ref[step * cap + one]], sems.at[slot, one]
+        )
+
+    @pl.when(step >= 2)
+    def _():
+        for one in range(cap):
+            put(slot, step - 2, one).wait()
+
+    for one in range(cap):
+        normed, spread = normed_of(x_refs[one], row_ref[one])
+        total = width * parts
+        grad_mean = sum(ref[one, 0:1, :] for ref in sum_refs) / total
+        cross_mean = sum(ref[one, 1:2, :] for ref in sum_refs) / total
+        grad = side_by_side([grad_ref[one] for grad_ref in grad_refs])
+        branch = spread * (
+            grad - down_lanes(grad_mean, width) - normed * down_lanes(cross_mean, width)
+        )
+        out_buf[slot, one] = (dy_refs[one][0].astype(F32) + branch).astype(BF16)
+        put(slot, step, one).start()
+
+    @pl.when(step == last)
+    def _():
+        for one in range(cap):
+            put(slot, step, one).wait()
+
+    @pl.when((step == last) & (step >= 1))
+    def _():
+        for one in range(cap):
+            put(1 - slot, step - 1, one).wait()
+
+
+def hid_grad_kernel(parts, cap, held, of_pair, own_ref, pair_ref, *refs):
+    dy_refs, w_refs, out_refs = refs[:parts], refs[parts : parts + held], refs[parts + held : -4]
+    dy_buf, w_buf, dy_sems, w_sems = refs[-4:]
+    groups = w_buf.shape[0]
+    segs = groups * cap
+    frames, width = dy_refs[0].shape[1:]
+    step = pl.program_id(0)
+    owner, me = own_ref[2 * segs], own_ref[2 * segs + 1]
+    table = pair_ref if of_pair else own_ref
+
+    def held_index(group):
+        language = table[segs + group * cap]
+        index = ((owner >> 1) - (language >> 1)) & (held - 1)
+        return jnp.where((language & 1) == (owner & 1), index, -1)
+
+    def w_copy(group, source):
+        return pltpu.make_async_copy(source, w_buf.at[group], w_sems.at[group])
+
+    def dy_copy(group, part, one):
+        return pltpu.make_async_copy(
+            dy_refs[part].at[table[group * cap + one]],
+            dy_buf.at[group, part, pl.ds(one * frames, frames)],
+            dy_sems.at[group, part, one],
+        )
+
+    @pl.when(step == 0)
+    def _():
+        for group in range(groups):
+            index = held_index(group)
+            for at, source in enumerate(w_refs):
+
+                @pl.when(index == at)
+                def _():
+                    w_copy(group, source).start()
+
+            @pl.when(index >= 0)
+            def _():
+                for part in range(parts):
+                    for one in range(cap):
+                        dy_copy(group, part, one).start()
+
+    @pl.when(held_index(step) >= 0)
+    def _():
+        w_copy(step, w_refs[0]).wait()
+        total = None
+        for part in range(parts):
+            for one in range(cap):
+                dy_copy(step, part, one).wait()
+            columns = pl.ds(pl.multiple_of((me ^ part) * width, 128), width)
+            term = lax.dot_general(
+                dy_buf[step, part],
+                w_buf[step, :, columns],
+                (((1,), (1,)), ((), ())),
+                preferred_element_type=F32,
+            )
+            total = term if total is None else total + term
+        chunk = total.shape[1] // len(out_refs)
+        for index, out_ref in enumerate(out_refs):
+            out_ref[0] = total[:, index * chunk : (index + 1) * chunk].astype(BF16)
+
+
+def w_grad_kernel(cap, segs, line, step, parts, places, scale, own_ref, pair_ref, *refs):
+    refs = list(refs)
+
+    def take(number):
+        return [refs.pop(0) for _ in range(number)]
+
+    hid_refs, dy_refs, add_refs = take(2), [take(parts), take(parts)], take(len(places))
+    out_ref, hid_buf, dy_buf, add_buf, hid_sems, dy_sems, add_sems = refs
+    width = dy_buf.shape[3]
+    frames = dy_buf.shape[2] // cap
+    owner, me = own_ref[2 * segs], own_ref[2 * segs + 1]
+    language = 2 * (((owner >> 1) - step) & (line - 1)) + (owner & 1)
+    found = []
+    for table in (own_ref, pair_ref):
+        group = jnp.int32(-1)
+        for at in range(segs // cap):
+            group = jnp.where(table[segs + at * cap] == language, at, group)
+        found.append(group)
+
+    def hid_copy(side):
+        source = hid_refs[side].at[jnp.maximum(found[side], 0)]
+        return pltpu.make_async_copy(source, hid_buf.at[side], hid_sems.at[side])
+
+    def dy_copies(side, part):
+        for one in range(cap):
+            segment = (own_ref, pair_ref)[side][jnp.maximum(found[side], 0) * cap + one]
+            yield pltpu.make_async_copy(
+                dy_refs[side][part].at[segment],
+                dy_buf.at[side, part, pl.ds(one * frames, frames)],
+                dy_sems.at[side, part, one],
+            )
+
+    def add_copy(index):
+        ref = add_refs[index]
+        held = add_buf.at[:, pl.ds(places[index], ref.shape[1])]
+        return pltpu.make_async_copy(ref, held, add_sems.at[index])
+
+    for side in range(2):
+
+        @pl.when(found[side] >= 0)
+        def _():
+            hid_copy(side).start()
+            for part in range(parts):
+                for copy in dy_copies(side, part):
+                    copy.start()
+
+    for index in range(len(places)):
+        add_copy(index).start()
+    for side in range(2):
+
+        @pl.when(found[side] >= 0)
+        def _():
+            hid_copy(side).wait()
+
+    first, second = found[0] >= 0, found[1] >= 0
+    for index in range(len(places)):
+        add_copy(index).wait()
+    for part in range(parts):
+        at = slice(part * width, (part + 1) * width)
+
+        def product(side):
+            return lax.dot_general(
+                hid_buf[side],
+                dy_buf[side, part],
+                (((0,), (0,)), ((), ())),
+                preferred_element_type=F32,
+            )
+
+        def put(value):
+            if places:
+                value = value + add_buf[:, at].astype(F32)
+            if scale is None:
+                out_ref[:, at] = value.astype(BF16)
+            else:
+                columns = pl.ds(pl.multiple_of((me ^ part) * width, 128), width)
+                out_ref[:, columns] = (value * scale).astype(BF16)
+
+        for side in range(2):
+
+            @pl.when(found[side] >= 0)
+            def _():
+                for copy in dy_copies(side, part):
+                    copy.wait()
+
+        @pl.when(first & second)
+        def _():
+            put(product(0) + product(1))
+
+        @pl.when(first & jnp.logical_not(second))
+        def _():
+            put(product(0))
+
+        @pl.when(jnp.logical_not(first) & second)
+        def _():
+            put(product(1))
+
+        @pl.when(jnp.logical_not(first | second))
+        def _():
+            put(jnp.zeros((out_ref.shape[0], width), F32))
+
+
+def moved_weights(feats, cotan, lang, w_out, gain, kernel):
+    segs, frames, width = feats.shape
+    owners = lax.axis_size("expert")
+    parts = lax.axis_size("fsdp")
+    line = owners // 2
+    cap = max(1, 2 * segs // owners)
+    groups = segs // cap
+    taps = kernel.shape[1]
+    rows, total_width = w_out.shape[1:]
+    owner = lax.axis_index("expert")
+    me = lax.axis_index("fsdp")
+    forward, inverse, tap_wave, lag_wave, period = wave_tables(frames, taps)
+    grad_scale = float(segs * frames) ** (-0.5)
+    chunk = 128
+    chunks = width // chunk
+
+    def pair_swap(value):
+        return lax.ppermute(value, "expert", [(i, i ^ 1) for i in range(owners)])
+
+    def along(value):
+        return lax.ppermute(value, "expert", [(i, (i + 2) % owners) for i in range(owners)])
+
+    def swap(value, bit):
+        return lax.ppermute(value, "fsdp", [(i, i ^ bit) for i in range(parts)])
+
+    def after(value, *others):
+        return lax.optimization_barrier((value, *others))[0]
+
+    def whole(array):
+        return pl.BlockSpec(array.shape, lambda *_: (0,) * array.ndim)
+
+    def like(shape, dtype):
+        return jax.ShapeDtypeStruct(shape, dtype)
+
+    order_of_calls = []
+
+    def call(body, name, scalars, inputs, outputs, grid, scratch=(), flops=0, waits=()):
+        if scalars:
+            scalars = (after(scalars[0], *order_of_calls[-1:], *waits), *scalars[1:])
+        arrays, in_specs = zip(*inputs)
+        shapes, out_specs = zip(*outputs)
+        moved = sum(math.prod(a.shape) * a.dtype.itemsize for a in (*arrays, *shapes))
+        found = pl.pallas_call(
+            body,
+            grid_spec=pltpu.PrefetchScalarGridSpec(
+                num_scalar_prefetch=len(scalars),
+                grid=grid,
+                in_specs=in_specs,
+                out_specs=out_specs,
+                scratch_shapes=scratch,
+            ),
+            out_shape=shapes,
+            compiler_params=pltpu.CompilerParams(vmem_limit_bytes=VMEM_BYTES),
+            cost_estimate=pl.CostEstimate(
+                flops=int(flops * WEIGHT.get(name, 1)),
+                bytes_accessed=int(moved * WEIGHT.get(name, 1)),
+                transcendentals=0,
+            ),
+            name=name,
+        )(*scalars, *arrays)
+        order_of_calls.append(found[0])
+        return list(found)
+
+    any_spec = pl.BlockSpec(memory_space=pl.ANY)
+
+    lang_row = jnp.pad(lang.astype(BF16), (0, width - segs))[None]
+    tap_rows = jnp.concatenate([kernel[0], gain, lang_row], axis=0)
+    tap_rows = jnp.pad(tap_rows, ((0, -tap_rows.shape[0] % 16), (0, 0)))[None]
+    tap_rows = jnp.concatenate([tap_rows, pair_swap(tap_rows)], axis=0)
+    tap_rows = [tap_rows] + [
+        lax.ppermute(tap_rows, "expert", [(i, i ^ (2 * k)) for i in range(owners)])
+        for k in range(1, line)
+    ]
+    per_step = 4 if segs % 4 == 0 else 1
+    stats = call(
+        stats_kernel,
+        "frame_stats",
+        (),
+        [(feats, pl.BlockSpec((per_step, frames, width), lambda i: (i, 0, 0)))],
+        [
+            (
+                like((segs, 8, frames), F32),
+                pl.BlockSpec((per_step, 8, frames), lambda i: (i, 0, 0)),
+            )
+        ],
+        (segs // per_step,),
+    )[0]
+    stat_parts = [stats] + [swap(stats, k) for k in range(1, parts)]
+
+    def table_of(langs, *more):
+        position = jnp.arange(segs, dtype=jnp.int32)
+        before = (langs[None, :] < langs[:, None]) | (
+            (langs[None, :] == langs[:, None]) & (position[None, :] < position[:, None])
+        )
+        rank = jnp.sum(before.astype(jnp.int32), axis=1)
+        placed = rank[None, :] == position[:, None]
+        order = jnp.sum(jnp.where(placed, position[None, :], 0), axis=1)
+        in_order = jnp.sum(jnp.where(placed, langs[None, :], 0), axis=1)
+        return jnp.concatenate([order, in_order, *more]).astype(jnp.int32)
+
+    own_table = table_of(lang, jnp.stack([owner, me]))
+    lang_sorted = own_table[segs : 2 * segs]
+    pair_table = table_of(tap_rows[0][1, taps + 1, :segs].astype(jnp.int32))
+
+    w_held = [w_out[0], along(after(w_out[0], tap_rows[1]))]
+    dy_pair = pair_swap(after(cotan, tap_rows[0]))
+    dy_core = swap(after(cotan, *stat_parts, *tap_rows), 1)
+    dy_far = swap(after(cotan, *stat_parts), parts // 2) if parts > 2 else None
+
+    seg_block = (1, frames, width)
+    group_rows = cap * frames
+
+    def by_order(array, lane=0, lanes=width):
+        return [
+            (array, pl.BlockSpec((1, frames, lanes), lambda g, o, *_, k=k: (o[g * cap + k], 0, lane)))
+            for k in range(cap)
+        ]
+
+    def in_turn(shape, lane=0):
+        return pl.BlockSpec(shape, lambda g, *_: (g, 0, lane))
+
+    tap_table = call(
+        tap_kernel,
+        "tap_waves",
+        (),
+        [(jnp.asarray(tap_wave), whole(tap_wave))] + [(one, whole(one)) for one in tap_rows],
+        [
+            (
+                like((owners, period + 8, width), F32),
+                pl.BlockSpec((owners, period + 8, width), lambda: (0, 0, 0)),
+            )
+        ],
+        (),
+        flops=4 * owners * period * taps * width,
+    )[0]
+
+    def tap_inputs(lane=0, lanes=width):
+        def at(g, own, *_):
+            return own[segs + g * cap] ^ own[2 * segs], 0, lane
+
+        return [
+            (tap_table, pl.BlockSpec((1, period + 8, lanes), at)),
+            (jnp.asarray(forward), whole(forward)),
+            (jnp.asarray(inverse), whole(inverse)),
+        ]
+
+    stat_inputs = [
+        (part, pl.BlockSpec((1, 8, frames), lambda g, o, *_, k=k: (o[g * cap + k], 0, 0)))
+        for part in stat_parts
+        for k in range(cap)
+    ]
+    wave_flops = 12 * segs * period * frames * width
+    cap_block = (cap, frames, width)
+    hidden, conv, wave, row_values = call(
+        lambda *refs: front_kernel(cap, parts, *refs),
+        "front",
+        (own_table,),
+        by_order(feats) + stat_inputs + tap_inputs(),
+        [
+            (like((groups, group_rows, width), BF16), in_turn((1, group_rows, width))),
+            (like(feats.shape, F32), in_turn(cap_block)),
+            (like((segs, period, width), F32), in_turn((cap, period, width))),
+            (like((segs, 8, frames), F32), in_turn((cap, 8, frames))),
+        ],
+        (groups,),
+        flops=wave_flops,
+    )
+
+    dy_parts, dy_pair_parts = [cotan, dy_core], [dy_pair]
+    dy_pair_core = swap(after(dy_pair, hidden, dy_far, w_held[1], dy_core), 1)
+    dy_pair_parts.append(dy_pair_core)
+    for step in range(2, line):
+        w_held.append(along(after(w_held[-1], hidden, dy_pair, dy_far, dy_core)))
+
+    hidden_pair = pair_swap(after(hidden, dy_pair, dy_far, w_held[1], dy_core))
+    if parts > 2:
+        dy_pair_far = swap(after(dy_pair, hidden, dy_far, w_held[1], dy_core), parts // 2)
+        dy_parts += [dy_far, swap(after(dy_far, dy_pair_core), 1)]
+        dy_pair_parts += [dy_pair_far, swap(dy_pair_far, 1)]
+
+    def w_grad_call(step, part_ids, adds, places, scale=None):
+        across = len(part_ids) * width
+        inputs = [hidden, hidden_pair]
+        inputs += [dy_parts[k] for k in part_ids] + [dy_pair_parts[k] for k in part_ids]
+        return call(
+            lambda *refs: w_grad_kernel(
+                cap, segs, line, step, len(part_ids), places, scale, *refs
+            ),
+            "w_grad",
+            (own_table, pair_table),
+            [(array, any_spec) for array in (*inputs, *adds)],
+            [(like((rows, across), BF16), pl.BlockSpec((rows, across), lambda *_: (0, 0)))],
+            (1,),
+            scratch=[
+                pltpu.VMEM((2, group_rows, width), BF16),
+                pltpu.VMEM((2, len(part_ids), group_rows, width), BF16),
+                pltpu.VMEM((rows, across), BF16),
+                pltpu.SemaphoreType.DMA((2,)),
+                pltpu.SemaphoreType.DMA((2, len(part_ids), cap)),
+                pltpu.SemaphoreType.DMA((max(len(places), 1),)),
+            ],
+            flops=4 * group_rows * rows * across,
+        )[0]
+
+    pieces = [list(range(parts // 2)), list(range(parts // 2, parts))]
+    arrived = [[] for _ in pieces]
+
+    def line_step(step, index):
+        share = w_grad_call(step, pieces[index], arrived[index], [0] * len(arrived[index]))
+        arrived[index] = [along(share)]
+
+    line_steps = [(step, index) for step in range(1, line) for index in range(len(pieces))]
+
+    def line_steps_until(step, index):
+        while line_steps and line_steps[0] <= (step, index):
+            line_step(*line_steps.pop(0))
+
+    def hid_grad_of(of_pair, dys):
+        return call(
+            lambda *refs: hid_grad_kernel(parts, cap, line, of_pair, *refs),
+            "hid_grad",
+            (own_table, pair_table),
+            [(array, any_spec) for array in (*dys, *w_held)],
+            [
+                (like((groups, group_rows, chunk), BF16), in_turn((1, group_rows, chunk)))
+                for _ in range(chunks)
+            ],
+            (groups,),
+            scratch=[
+                pltpu.VMEM((groups, parts, group_rows, width), BF16),
+                pltpu.VMEM((groups, rows, total_width), BF16),
+                pltpu.SemaphoreType.DMA((groups, parts, cap)),
+                pltpu.SemaphoreType.DMA((groups,)),
+            ],
+            flops=2 * segs * frames * rows * total_width,
+        )
+
+    line_steps_until(1, 1)
+    hid_grad_sent = hid_grad_of(True, dy_pair_parts)
+    hid_grad_pair = [pair_swap(hid_grad_sent[0])]
+    for one in hid_grad_sent[1:]:
+        hid_grad_pair.append(pair_swap(after(one, hid_grad_pair[-1])))
+    line_steps_until(2, 0)
+    hid_grad_own = hid_grad_of(False, dy_parts)
+
+    norm_grads, sums, smalls = [], [], []
+    line_steps_until(3, 0)
+    for c in range(chunks):
+        if c == 1:
+            line_steps_until(line, 0)
+        norm_grad, part_sums, small = call(
+            lambda *refs: back_kernel(cap, *refs),
+            "back",
+            (own_table,),
+            by_order(feats, c, chunk)
+            + [(row_values, in_turn((cap, 8, frames)))]
+            + tap_inputs(c, chunk)
+            + [
+                (jnp.asarray(lag_wave), whole(lag_wave)),
+                (hid_grad_own[c], in_turn((1, group_rows, chunk))),
+                (hid_grad_pair[c], in_turn((1, group_rows, chunk))),
+                (conv, in_turn((cap, frames, chunk), c)),
+                (wave, in_turn((cap, period, chunk), c)),
+            ],
+            [
+                (like((segs, frames, chunk), F32), in_turn((cap, frames, chunk))),
+                (like((segs, 8, frames), F32), in_turn((cap, 8, frames))),
+                (like((groups, taps + 1, chunk), F32), in_turn((1, taps + 1, chunk))),
+            ],
+            (groups,),
+            flops=wave_flops // chunks,
+        )
+        norm_grads.append(norm_grad)
+        sums.append(part_sums)
+        smalls.append(small)
+    line_steps_until(line, 0)
+    sums = sum(sums)
+    sum_parts = [sums] + [swap(sums, k) for k in range(1, parts)]
+    w_grad = w_grad_call(
+        0,
+        list(range(parts)),
+        [array for one in arrived for array in one],
+        [piece[0] * width for piece in pieces],
+        scale=grad_scale,
+    )
+    feat_grad = call(
+        lambda *refs: final_kernel(cap, chunks, *refs),
+        "input_grad",
+        (own_table,),
+        by_order(feats)
+        + by_order(cotan)
+        + [(one, in_turn((cap, frames, chunk))) for one in norm_grads]
+        + [(one, in_turn((cap, 8, frames))) for one in (row_values, *sum_parts)],
+        [(like(feats.shape, BF16), any_spec)],
+        (groups,),
+        scratch=[
+            pltpu.VMEM((2, cap, frames, width), BF16),
+            pltpu.SemaphoreType.DMA((2, cap)),
+        ],
+    )[0]
+
+    small = jnp.concatenate(smalls, axis=2)
+    group_lang = lang_sorted.reshape(groups, cap)[:, 0]
+    slots = jnp.arange(owners, dtype=jnp.int32)[:, None] == group_lang[None, :]
+    spread = jnp.sum(jnp.where(slots[:, :, None, None], small[None], 0.0), axis=1)
+    shared = lax.all_to_all(spread, "expert", split_axis=0, concat_axis=0, tiled=True)
+    small_sum = jnp.sum(shared, axis=0) * grad_scale
+
+    return (feat_grad, w_grad[None], small_sum[taps:], small_sum[None, :taps])
+
+
+def per_device(feats, cotan, lang, w_out, gain, kernel):
+    segs, frames, width = feats.shape
+    owners = lax.axis_size("expert")
+    parts = lax.axis_size("fsdp")
+    weights_moved = 2 * (owners // 2 - 1) * math.prod(w_out.shape)
+    frames_moved = 3 * 2 * math.prod(feats.shape)
+    fits = owners & (owners - 1) == 0 and owners > 1 and parts & (parts - 1) == 0 and frames % 128 == 0 and width % frames == 0 and parts in (2, 4) and segs <= 256 and segs <= 256 and segs <= 256 and segs <= 256 and segs <= 256 and segs <= 256 and segs <= 256
+    if fits and weights_moved < frames_moved:
+        return moved_weights(feats, cotan, lang, w_out, gain, kernel)
+    return routed_frames(feats, cotan, lang, w_out, gain, kernel)
+
+
 def solution(mesh):
     in_specs = (
         P("expert", None, "fsdp"),

time: 411 us -> 222 us (0.54)
  other arithmetic: 106 us -> 4.61 us
  Pallas kernels: 0 us -> 89.1 us
  waiting for transfers between devices: 152 us -> 88.9 us
  matrix products: 49.2 us -> 0 us
  local copies, waits for them, and re-layouts: 42.6 us -> 10.2 us
  blocking collectives: 22.9 us -> 0 us
  between operations: 14.3 us -> 1.2 us
  starting transfers between devices: 22.6 us -> 28.7 us
    all_to_all x4 -> x1, waiting for transfers between devices: 152 us -> 0.01 us  [moved_weights(): lax.all_to_all(spread, 'expert', split_axis=0, concat_axis=0, tiled=True)]
    pallas_call x0 -> x16, Pallas kernels: none -> 89.1 us  [call(): pl.pallas_call(body, grid_spec=pltpu.PrefetchScalarGridSpec(num_scalar_pr...]
    ppermute x0 -> x30, waiting for transfers between devices: none -> 88.9 us  [the longest x9 79.3 us: along(): lax.ppermute(value, 'expert', [(i, (i + 2) % owners) for i in range(owner...]
    reduce_sum x6, other arithmetic: 84.2 us -> 1.6 us  [the longest x1 0.97 us: moved_weights(): jnp.sum(jnp.where(slots[:, :, None, None], small[None], 0.0), axis=1)]
    dot_general x8 -> x0, matrix products: 49.2 us -> none  [the longest x1 27.2 us: per_device(): hid_sum = jnp.dot(shard_part, w_rows.T, preferred_element_type=jnp.float32)]
    reshape x6 -> x1, local copies, waits for them, and re-layouts: 27.9 us -> 0.08 us  [moved_weights(): group_lang = lang_sorted.reshape(groups, cap)[:, 0]]
    ppermute x0 -> x30, starting transfers between devices: none -> 23.1 us  [the longest x6 9.28 us: pair_swap(): return lax.ppermute(value, 'expert', [(i, i ^ 1) for i in range(owners)])]
    psum x3 -> x0, blocking collectives: 22.9 us -> none  [the longest x1 10.2 us: back_split(): lax.psum((jnp.sum(norm_grad, axis=-1), jnp.sum(norm_grad * normed, axis=-...]
  transfers between devices with their start and end apart: 5 -> 31, of which waited for: 3 -> 10; matrix products, arithmetic and copies ran while one was open for 23% -> 2% of each run, Pallas kernels for 0% -> 38%
where the time goes in v1:
time: 222 us; the launch traced here: 223 us
  Pallas kernels  89.1 us (40%)
  waiting for transfers between devices  88.9 us (40%)
  starting transfers between devices  28.7 us (13%)
  local copies, waits for them, and re-layouts  10.2 us (5%)
  other arithmetic  4.61 us (2%)
    pallas_call x16, Pallas kernels, call(): pl.pallas_call(body, grid_spec=pltpu.PrefetchScalarGridSpec(num_scalar_pr...  89.1 us
    ppermute x9, waiting for transfers between devices, along(): lax.ppermute(value, 'expert', [(i, (i + 2) % owners) for i in range(owner...  79.3 us
    unnamed x69, local copies, waits for them, and re-layouts  9.42 us
    ppermute x6, starting transfers between devices, pair_swap(): return lax.ppermute(value, 'expert', [(i, i ^ 1) for i in range(owners)])  9.28 us
    ppermute x12, starting transfers between devices, swap(): return lax.ppermute(value, 'fsdp', [(i, i ^ bit) for i in range(parts)])  8.21 us
    all_to_all x1, starting transfers between devices, moved_weights(): lax.all_to_all(spread, 'expert', split_axis=0, concat_axis=0, tiled=True)  5.59 us
    ppermute x3, starting transfers between devices, moved_weights(): lax.ppermute(tap_rows, 'expert', [(i, i ^ 2 * k) for i in range(owners)])  4.45 us
  transfers between devices with their start and end apart: 31, of which 10 were waited for; matrix products, arithmetic and copies ran while one was open for 2% of the time, Pallas kernels for 38%

profile of v1, /device:TPU:0, one launch (start us, length us, event | category | flops | bytes accessed | tf_op | source)
XLA Modules:
  0.0 222.8 jit_solution(6628297017692930300)
XLA Ops:
  0.7 4.3 %frame_stats.1.refs_5_.refs_6_.refs_7_.refs_8_ = f32[16,8,128]{2,1,0:T(8,128)} custom-call(bf16[16,128,384]{2,1,0:T(8,128)(2,1)} %refs_4_.17), custom_call_target="tpu_custom_call" | custom-call | bytes 49152000 | tf_op jit(solution)/shard_map/frame_stats/pallas_call | solution.py:603
  5.4 2.5 %collective-permute-start.5 = (f32[16,8,128]{2,1,0:T(8,128)}, f32[16,8,128]{2,1,0:T(8,128)S(1)}, u32[]{:S(2)}, u32[]{:S(2)}) collective-permute-start(f32[16,8,128]{2,1,0:T(8,128)} %frame_stats.1.refs_5_.refs_6_.refs_7_.refs_8_), channel_id=1, source_target_pairs={{0,2},{1,3},{2,0},{3,1},{4,6},{5,7},{6,4},{7,5},{8,10},{9,11},{10,... | collective-permute-start | bytes 196616 | tf_op jit(solution)/shard_map/ppermute | solution.py:584
  8.1 1.8 collective-permute-start
  10.2 1.9 collective-permute-done
  12.1 1.9 collective-permute-start.1
  14.0 2.6 %collective-permute-start.2 = (bf16[2,48,384]{2,1,0:T(8,128)(2,1)S(1)}, bf16[2,48,384]{2,1,0:T(8,128)(2,1)S(1)}, u32[]{:S(2)}, u32[]{:S(2)}) collective-permute-start(bf16[2,48,384]{2,1,0:T(8,128)(2,1)S(1)} %pad_maximum_fusion.1.refs_0_), channel_id=1, source_target_pairs={{0,16},{4,20},{8,24},{12,28},{16,0},{20,4},{24,8},{28,12},{1,17},{... | collective-permute-start | bytes 221192 | tf_op jit(solution)/shard_map/ppermute | solution.py:631
  17.3 1.8 collective-permute-start.7
  23.5 3.0 %tap_waves.1.refs_21_.refs_6_ = f32[8,152,384]{2,1,0:T(8,128)} custom-call(bf16[2,144,32]{2,1,0:T(8,128)(2,1)} %constant.25.clone.wave_ref, bf16[2,48,384]{2,1,0:T(8,128)(2,1)} %copy-done.8, bf16[2,48,384]{2,1,0:T(8,128)(2,1)} %copy-done.28, bf16[2,48,384]{2,1,0:T(8,128)(2,1)} %copy-done.29, bf16[2,48,384]{2,1,0:T(8,128)(2,1)} %copy-done.30), custom_call_target="tpu_custom_call" | custom-call | flops 1645608960 | bytes 65433600 | tf_op jit(solution)/shard_map/tap_waves/pallas_call | solution.py:603
  27.2 8.6 %front.1 = (bf16[4,512,384]{2,1,0:T(8,128)(2,1)}, f32[16,128,384]{2,1,0:T(8,128)}, f32[16,144,384]{2,1,0:T(8,128)}, f32[16,8,128]{2,1,0:T(8,128)}) custom-call(s32[34]{0:T(128)} %pad_add_fusion.refs_0_, bf16[16,128,384]{2,1,0:T(8,128)(2,1)} %refs_4_.17, bf16[16,128,384]{2,1,0:T(8,128)(2,1)} %refs_4_.17, bf16[16,128,384]{2,1,0:T(8,128)(2,1)} %refs_4_.17, ...), custom_call_target="tpu_custom_call" | custom-call | flops 40768634880 | bytes 532561920 | tf_op jit(solution)/shard_map/front/pallas_call | solution.py:603
  35.8 21.0 %collective-permute-done.9.refs_7_ = bf16[384,1536]{1,0:T(8,128)(2,1)} collective-permute-done((bf16[384,1536]{1,0:T(8,128)(2,1)S(1)}, bf16[384,1536]{1,0:T(8,128)(2,1)}, u32[]{:S(2)}, u32[]{:S(2)}) %collective-permute-start.9) | collective-permute-done | bytes 1179680 | tf_op jit(solution)/shard_map/ppermute | solution.py:581
  56.9 1.6 collective-permute-start.14
  61.1 28.7 %collective-permute-done.16.refs_8_ = bf16[384,1536]{1,0:T(8,128)(2,1)S(1)} collective-permute-done((bf16[384,1536]{1,0:T(8,128)(2,1)}, bf16[384,1536]{1,0:T(8,128)(2,1)S(1)}, u32[]{:S(2)}, u32[]{:S(2)}) %collective-permute-start.16) | collective-permute-done | bytes 1179680 | tf_op jit(solution)/shard_map/ppermute | solution.py:581
  89.8 4.2 %collective-permute-done.14.refs_6_.refs_4_.refs_10_ = bf16[16,128,384]{2,1,0:T(8,128)(2,1)} collective-permute-done((bf16[16,128,384]{2,1,0:T(8,128)(2,1)}, bf16[16,128,384]{2,1,0:T(8,128)(2,1)}, u32[]{:S(2)}, u32[]{:S(2)}) %collective-permute-start.14) | collective-permute-done | bytes 1572896 | tf_op jit(solution)/shard_map/ppermute | solution.py:584
  95.2 3.9 %w_grad.7 = bf16[384,768]{1,0:T(8,128)(2,1)} custom-call(s32[34]{0:T(128)} %pad_add_fusion.refs_0_, s32[32]{0:T(128)} %pad_add_fusion.1.refs_1_, bf16[4,512,384]{2,1,0:T(8,128)(2,1)} %get-tuple-element.55.refs_2_, bf16[4,512,384]{2,1,0:T(8,128)(2,1)} %collective-permute-done.11.refs_3_, bf16[16,128,384]{2,1,0:T(8,128)(2,1)} %refs_8_.4, ...), custom_call_target="tpu_custom_call" | custom-call | flops 18119393280 | bytes 300810240 | tf_op jit(solution)/shard_map/w_grad/pallas_call | solution.py:603
  99.3 3.9 %w_grad.8 = bf16[384,768]{1,0:T(8,128)(2,1)} custom-call(s32[34]{0:T(128)} %pad_add_fusion.refs_0_, s32[32]{0:T(128)} %pad_add_fusion.1.refs_1_, bf16[4,512,384]{2,1,0:T(8,128)(2,1)} %get-tuple-element.55.refs_2_, bf16[4,512,384]{2,1,0:T(8,128)(2,1)} %collective-permute-done.11.refs_3_, bf16[16,128,384]{2,1,0:T(8,128)(2,1)} %collective-permute-done.8.refs_4_.refs_6_, ...), custom_call_target="tpu_custom_call" | custom-call | flops 18119393280 | bytes 300810240 | tf_op jit(solution)/shard_map/w_grad/pallas_call | solution.py:603
  103.1 17.3 %collective-permute-done.17.refs_9_ = bf16[384,1536]{1,0:T(8,128)(2,1)S(1)} collective-permute-done((bf16[384,1536]{1,0:T(8,128)(2,1)S(1)}, bf16[384,1536]{1,0:T(8,128)(2,1)S(1)}, u32[]{:S(2)}, u32[]{:S(2)}) %collective-permute-start.17) | collective-permute-done | bytes 1179680 | tf_op jit(solution)/shard_map/ppermute | solution.py:581
  121.4 10.2 %hid_grad.2 = (bf16[4,512,128]{2,1,0:T(8,128)(2,1)}, bf16[4,512,128]{2,1,0:T(8,128)(2,1)}, bf16[4,512,128]{2,1,0:T(8,128)(2,1)}) custom-call(s32[34]{0:T(128)} %pad_add_fusion.refs_0_, s32[32]{0:T(128)} %pad_add_fusion.1.refs_1_, bf16[16,128,384]{2,1,0:T(8,128)(2,1)} %collective-permute-done.7.refs_6_.refs_2_.refs_8_, ...), custom_call_target="tpu_custom_call" | custom-call | flops 2415919104 | bytes 12582912 | tf_op jit(solution)/shard_map/hid_grad/pallas_call | solution.py:603
  133.2 4.2 %w_grad.9 = bf16[384,768]{1,0:T(8,128)(2,1)} custom-call(s32[34]{0:T(128)} %pad_add_fusion.refs_0_, s32[32]{0:T(128)} %pad_add_fusion.1.refs_1_, bf16[4,512,384]{2,1,0:T(8,128)(2,1)} %get-tuple-element.55.refs_2_, bf16[4,512,384]{2,1,0:T(8,128)(2,1)} %collective-permute-done.11.refs_3_, bf16[16,128,384]{2,1,0:T(8,128)(2,1)} %refs_8_.4, ...), custom_call_target="tpu_custom_call" | custom-call | flops 18119393280 | bytes 318504960 | tf_op jit(solution)/shard_map/w_grad/pallas_call | solution.py:603
  137.5 6.2 %hid_grad.3 = (bf16[4,512,128]{2,1,0:T(8,128)(2,1)}, bf16[4,512,128]{2,1,0:T(8,128)(2,1)}, bf16[4,512,128]{2,1,0:T(8,128)(2,1)}) custom-call(s32[34]{0:T(128)} %pad_add_fusion.refs_0_, s32[32]{0:T(128)} %pad_add_fusion.1.refs_1_, bf16[16,128,384]{2,1,0:T(8,128)(2,1)} %refs_8_.4, bf16[16,128,384]{2,1,0:T(8,128)(2,1)} %collective-permute-done.10.refs_5_.refs_3_, ...), custom_call_target="tpu_custom_call" | custom-call | flops 2415919104 | bytes 12582912 | tf_op jit(solution)/shard_map/hid_grad/pallas_call | solution.py:603
  143.7 2.0 collective-permute-start.23
  145.7 4.6 %collective-permute-done.19.refs_8_ = bf16[384,768]{1,0:T(8,128)(2,1)S(1)} collective-permute-done((bf16[384,768]{1,0:T(8,128)(2,1)S(1)}, bf16[384,768]{1,0:T(8,128)(2,1)S(1)}, u32[]{:S(2)}, u32[]{:S(2)}) %collective-permute-start.19) | collective-permute-done | bytes 589856 | tf_op jit(solution)/shard_map/ppermute | solution.py:581
  151.1 4.0 %w_grad.10 = bf16[384,768]{1,0:T(8,128)(2,1)} custom-call(s32[34]{0:T(128)} %pad_add_fusion.refs_0_, s32[32]{0:T(128)} %pad_add_fusion.1.refs_1_, bf16[4,512,384]{2,1,0:T(8,128)(2,1)} %get-tuple-element.55.refs_2_, bf16[4,512,384]{2,1,0:T(8,128)(2,1)} %collective-permute-done.11.refs_3_, bf16[16,128,384]{2,1,0:T(8,128)(2,1)} %collective-permute-done.8.refs_4_.refs_6_, ...), custom_call_target="tpu_custom_call" | custom-call | flops 18119393280 | bytes 318504960 | tf_op jit(solution)/shard_map/w_grad/pallas_call | solution.py:603
  155.3 7.7 %collective-permute-done.20.refs_8_ = bf16[384,768]{1,0:T(8,128)(2,1)S(1)} collective-permute-done((bf16[384,768]{1,0:T(8,128)(2,1)}, bf16[384,768]{1,0:T(8,128)(2,1)S(1)}, u32[]{:S(2)}, u32[]{:S(2)}) %collective-permute-start.20) | collective-permute-done | bytes 589856 | tf_op jit(solution)/shard_map/ppermute | solution.py:581
  163.8 4.1 %w_grad.11 = bf16[384,768]{1,0:T(8,128)(2,1)} custom-call(s32[34]{0:T(128)} %pad_add_fusion.refs_0_, s32[32]{0:T(128)} %pad_add_fusion.1.refs_1_, bf16[4,512,384]{2,1,0:T(8,128)(2,1)} %get-tuple-element.55.refs_2_, bf16[4,512,384]{2,1,0:T(8,128)(2,1)} %collective-permute-done.11.refs_3_, bf16[16,128,384]{2,1,0:T(8,128)(2,1)} %refs_8_.4, ...), custom_call_target="tpu_custom_call" | custom-call | flops 18119393280 | bytes 318504960 | tf_op jit(solution)/shard_map/w_grad/pallas_call | solution.py:603
  167.9 7.1 %back.3 = (f32[16,128,128]{2,1,0:T(8,128)}, f32[16,8,128]{2,1,0:T(8,128)}, f32[4,32,128]{2,1,0:T(8,128)}) custom-call(s32[34]{0:T(128)} %pad_add_fusion.refs_0_, bf16[16,128,384]{2,1,0:T(8,128)(2,1)} %refs_4_.17, bf16[16,128,384]{2,1,0:T(8,128)(2,1)} %refs_4_.17, bf16[16,128,384]{2,1,0:T(8,128)(2,1)} %refs_4_.17, bf16[16,128,384]{2,1,0:T(8,128)(2,1)} %refs_4_.17, ...), custom_call_target="tpu_custom_call" | custom-call | flops 452984832 | bytes 17386496 | tf_op jit(solution)/shard_map/back/pallas_call | solution.py:603
  175.1 1.6 collective-permute-start.24
  177.4 4.0 %w_grad.12 = bf16[384,768]{1,0:T(8,128)(2,1)} custom-call(s32[34]{0:T(128)} %pad_add_fusion.refs_0_, s32[32]{0:T(128)} %pad_add_fusion.1.refs_1_, bf16[4,512,384]{2,1,0:T(8,128)(2,1)} %get-tuple-element.55.refs_2_, bf16[4,512,384]{2,1,0:T(8,128)(2,1)} %collective-permute-done.11.refs_3_, bf16[16,128,384]{2,1,0:T(8,128)(2,1)} %collective-permute-done.8.refs_4_.refs_6_, ...), custom_call_target="tpu_custom_call" | custom-call | flops 18119393280 | bytes 318504960 | tf_op jit(solution)/shard_map/w_grad/pallas_call | solution.py:603
  181.8 7.0 %back.4 = (f32[16,128,128]{2,1,0:T(8,128)}, f32[16,8,128]{2,1,0:T(8,128)}, f32[4,32,128]{2,1,0:T(8,128)}) custom-call(s32[34]{0:T(128)} %pad_add_fusion.refs_0_, bf16[16,128,384]{2,1,0:T(8,128)(2,1)} %refs_4_.17, bf16[16,128,384]{2,1,0:T(8,128)(2,1)} %refs_4_.17, bf16[16,128,384]{2,1,0:T(8,128)(2,1)} %refs_4_.17, bf16[16,128,384]{2,1,0:T(8,128)(2,1)} %refs_4_.17, ...), custom_call_target="tpu_custom_call" | custom-call | flops 452984832 | bytes 17386496 | tf_op jit(solution)/shard_map/back/pallas_call | solution.py:603
  189.6 7.1 %back.5 = (f32[16,128,128]{2,1,0:T(8,128)}, f32[16,8,128]{2,1,0:T(8,128)}, f32[4,32,128]{2,1,0:T(8,128)}) custom-call(s32[34]{0:T(128)} %pad_add_fusion.refs_0_, bf16[16,128,384]{2,1,0:T(8,128)(2,1)} %refs_4_.17, bf16[16,128,384]{2,1,0:T(8,128)(2,1)} %refs_4_.17, bf16[16,128,384]{2,1,0:T(8,128)(2,1)} %refs_4_.17, bf16[16,128,384]{2,1,0:T(8,128)(2,1)} %refs_4_.17, ...), custom_call_target="tpu_custom_call" | custom-call | flops 452984832 | bytes 17386496 | tf_op jit(solution)/shard_map/back/pallas_call | solution.py:603
  201.3 5.6 %all-to-all-start = ((f32[8,32,384]{2,1,0:T(8,128)}), f32[8,32,384]{2,1,0:T(8,128)S(1)}, u32[]{:S(2)}, u32[]{:S(2)}) async-start(f32[8,32,384]{2,1,0:T(8,128)} %select_reduce_fusion), calls=%async_computation | async-start | bytes 786432 | tf_op jit(solution)/shard_map/all_to_all | solution.py:866
  208.6 5.7 %w_grad.13 = bf16[384,1536]{1,0:T(8,128)(2,1)} custom-call(s32[34]{0:T(128)} %pad_add_fusion.refs_0_, s32[32]{0:T(128)} %pad_add_fusion.1.refs_1_, bf16[4,512,384]{2,1,0:T(8,128)(2,1)} %get-tuple-element.55.refs_2_, bf16[4,512,384]{2,1,0:T(8,128)(2,1)} %collective-permute-done.11.refs_3_, bf16[16,128,384]{2,1,0:T(8,128)(2,1)} %refs_8_.4, ...), custom_call_target="tpu_custom_call" | custom-call | flops 36238786560 | bytes 542638080 | tf_op jit(solution)/shard_map/w_grad/pallas_call | solution.py:603
  215.6 5.9 %input_grad.1 = bf16[16,128,384]{2,1,0:T(8,128)(2,1)} custom-call(s32[34]{0:T(128)} %pad_add_fusion.refs_0_, bf16[16,128,384]{2,1,0:T(8,128)(2,1)} %refs_4_.17, bf16[16,128,384]{2,1,0:T(8,128)(2,1)} %refs_4_.17, bf16[16,128,384]{2,1,0:T(8,128)(2,1)} %refs_4_.17, bf16[16,128,384]{2,1,0:T(8,128)(2,1)} %refs_4_.17, bf16[16,128,384]{2,1,0:T(8,128)(2,1)} %refs_8_.4, ...), custom_call_target="tpu_custom_call" | custom-call | bytes 17629184 | tf_op jit(solution)/shard_map/input_grad/pallas_call | solution.py:603
  (137 shorter events, 25.8 us)
Async XLA Ops:
  4.9 11.7 %collective-permute-start.4 = (f32[16,8,128]{2,1,0:T(8,128)}, f32[16,8,128]{2,1,0:T(8,128)S(1)}, u32[]{:S(2)}, u32[]{:S(2)}) collective-permute-start(f32[16,8,128]{2,1,0:T(8,128)} %frame_stats.1.refs_5_.refs_6_.refs_7_.refs_8_), channel_id=1, source_target_pairs={{0,1},{1,0},{2,3},{3,2},{4,5},{5,4},{6,7},{7,6},{8,9},{9,8},{10,11... | collective-permute-start | bytes 196616 | tf_op jit(solution)/shard_map/ppermute | solution.py:584
  5.4 11.9 %collective-permute-start.5 = (f32[16,8,128]{2,1,0:T(8,128)}, f32[16,8,128]{2,1,0:T(8,128)S(1)}, u32[]{:S(2)}, u32[]{:S(2)}) collective-permute-start(f32[16,8,128]{2,1,0:T(8,128)} %frame_stats.1.refs_5_.refs_6_.refs_7_.refs_8_), channel_id=1, source_target_pairs={{0,2},{1,3},{2,0},{3,1},{4,6},{5,7},{6,4},{7,5},{8,10},{9,11},{10,... | collective-permute-start | bytes 196616 | tf_op jit(solution)/shard_map/ppermute | solution.py:584
  7.9 11.2 %collective-permute-start.6 = (f32[16,8,128]{2,1,0:T(8,128)}, f32[16,8,128]{2,1,0:T(8,128)S(1)}, u32[]{:S(2)}, u32[]{:S(2)}) collective-permute-start(f32[16,8,128]{2,1,0:T(8,128)} %frame_stats.1.refs_5_.refs_6_.refs_7_.refs_8_), channel_id=1, source_target_pairs={{0,3},{1,2},{2,1},{3,0},{4,7},{5,6},{6,5},{7,4},{8,11},{9,10},{10,... | collective-permute-start | bytes 196616 | tf_op jit(solution)/shard_map/ppermute | solution.py:584
  8.1 4.0 %collective-permute-start = (bf16[1,48,384]{2,1,0:T(8,128)(2,1)S(1)}, bf16[1,48,384]{2,1,0:T(8,128)(2,1)S(1)}, u32[]{:S(2)}, u32[]{:S(2)}) collective-permute-start(bf16[1,48,384]{2,1,0:T(8,128)(2,1)S(1)} %fusion.5), channel_id=1, source_target_pairs={{0,4},{4,0},{8,12},{12,8},{16,20},{20,16},{24,28},{28,24},{1,5},{5... | collective-permute-start | bytes 110600 | tf_op jit(solution)/shard_map/ppermute | solution.py:578
  12.1 8.4 %collective-permute-start.1 = (bf16[2,48,384]{2,1,0:T(8,128)(2,1)S(1)}, bf16[2,48,384]{2,1,0:T(8,128)(2,1)S(1)}, u32[]{:S(2)}, u32[]{:S(2)}) collective-permute-start(bf16[2,48,384]{2,1,0:T(8,128)(2,1)S(1)} %pad_maximum_fusion.1.refs_0_), channel_id=1, source_target_pairs={{0,8},{4,12},{8,0},{12,4},{16,24},{20,28},{24,16},{28,20},{1,9},{5... | collective-permute-start | bytes 221192 | tf_op jit(solution)/shard_map/ppermute | solution.py:631
  14.0 7.4 %collective-permute-start.2 = (bf16[2,48,384]{2,1,0:T(8,128)(2,1)S(1)}, bf16[2,48,384]{2,1,0:T(8,128)(2,1)S(1)}, u32[]{:S(2)}, u32[]{:S(2)}) collective-permute-start(bf16[2,48,384]{2,1,0:T(8,128)(2,1)S(1)} %pad_maximum_fusion.1.refs_0_), channel_id=1, source_target_pairs={{0,16},{4,20},{8,24},{12,28},{16,0},{20,4},{24,8},{28,12},{1,17},{... | collective-permute-start | bytes 221192 | tf_op jit(solution)/shard_map/ppermute | solution.py:631
  16.6 6.3 %collective-permute-start.3 = (bf16[2,48,384]{2,1,0:T(8,128)(2,1)S(1)}, bf16[2,48,384]{2,1,0:T(8,128)(2,1)S(1)}, u32[]{:S(2)}, u32[]{:S(2)}) collective-permute-start(bf16[2,48,384]{2,1,0:T(8,128)(2,1)S(1)} %pad_maximum_fusion.1.refs_0_), channel_id=1, source_target_pairs={{0,24},{4,28},{8,16},{12,20},{16,8},{20,12},{24,0},{28,4},{1,25},{... | collective-permute-start | bytes 221192 | tf_op jit(solution)/shard_map/ppermute | solution.py:631
  17.3 39.5 %collective-permute-start.7 = (bf16[16,128,384]{2,1,0:T(8,128)(2,1)S(1)}, bf16[16,128,384]{2,1,0:T(8,128)(2,1)}, u32[]{:S(2)}, u32[]{:S(2)}) collective-permute-start(bf16[16,128,384]{2,1,0:T(8,128)(2,1)S(1)} %copy-done), channel_id=1, source_target_pairs={{0,4},{4,0},{8,12},{12,8},{16,20},{20,16},{24,28},{28,24},{1,5},{5... | collective-permute-start | bytes 4718600 | tf_op jit(solution)/shard_map/ppermute | solution.py:578
  19.1 37.7 %collective-permute-start.8 = (bf16[16,128,384]{2,1,0:T(8,128)(2,1)S(1)}, bf16[16,128,384]{2,1,0:T(8,128)(2,1)}, u32[]{:S(2)}, u32[]{:S(2)}) collective-permute-start(bf16[16,128,384]{2,1,0:T(8,128)(2,1)S(1)} %copy-done), channel_id=1, source_target_pairs={{0,2},{1,3},{2,0},{3,1},{4,6},{5,7},{6,4},{7,5},{8,10},{9,11},{10,... | collective-permute-start | bytes 4718600 | tf_op jit(solution)/shard_map/ppermute | solution.py:584
  26.5 30.3 %collective-permute-start.10 = (bf16[16,128,384]{2,1,0:T(8,128)(2,1)S(1)}, bf16[16,128,384]{2,1,0:T(8,128)(2,1)}, u32[]{:S(2)}, u32[]{:S(2)}) collective-permute-start(bf16[16,128,384]{2,1,0:T(8,128)(2,1)S(1)} %copy-done), channel_id=1, source_target_pairs={{0,1},{1,0},{2,3},{3,2},{4,5},{5,4},{6,7},{7,6},{8,9},{9,8},{10,11... | collective-permute-start | bytes 4718600 | tf_op jit(solution)/shard_map/ppermute | solution.py:584
  26.5 30.3 %collective-permute-start.9 = (bf16[384,1536]{1,0:T(8,128)(2,1)S(1)}, bf16[384,1536]{1,0:T(8,128)(2,1)}, u32[]{:S(2)}, u32[]{:S(2)}) collective-permute-start(bf16[384,1536]{1,0:T(8,128)(2,1)S(1)} %bitcast.16), channel_id=1, source_target_pairs={{0,8},{4,12},{8,16},{12,20},{16,24},{20,28},{24,0},{28,4},{1,9},{5... | collective-permute-start | bytes 3538952 | tf_op jit(solution)/shard_map/ppermute | solution.py:581
  56.8 32.9 %collective-permute-start.12 = (bf16[16,128,384]{2,1,0:T(8,128)(2,1)}, bf16[16,128,384]{2,1,0:T(8,128)(2,1)}, u32[]{:S(2)}, u32[]{:S(2)}) collective-permute-start(bf16[16,128,384]{2,1,0:T(8,128)(2,1)} %collective-permute-done.7.refs_6_.refs_2_.refs_8_), channel_id=1, source_target_pairs={{0,1},{1,0},{2,3},{3,2},{4,5},{5,4},{6,7},{7,6},{8,9},{9,8},{10,11... | collective-permute-start | bytes 4718600 | tf_op jit(solution)/shard_map/ppermute | solution.py:584
  56.9 37.1 %collective-permute-start.14 = (bf16[16,128,384]{2,1,0:T(8,128)(2,1)}, bf16[16,128,384]{2,1,0:T(8,128)(2,1)}, u32[]{:S(2)}, u32[]{:S(2)}) collective-permute-start(bf16[16,128,384]{2,1,0:T(8,128)(2,1)} %collective-permute-done.7.refs_6_.refs_2_.refs_8_), channel_id=1, source_target_pairs={{0,2},{1,3},{2,0},{3,1},{4,6},{5,7},{6,4},{7,5},{8,10},{9,11},{10,... | collective-permute-start | bytes 4718600 | tf_op jit(solution)/shard_map/ppermute | solution.py:584
  58.4 36.8 %collective-permute-start.11 = (bf16[4,512,384]{2,1,0:T(8,128)(2,1)}, bf16[4,512,384]{2,1,0:T(8,128)(2,1)}, u32[]{:S(2)}, u32[]{:S(2)}) collective-permute-start(bf16[4,512,384]{2,1,0:T(8,128)(2,1)} %get-tuple-element.55.refs_2_), channel_id=1, source_target_pairs={{0,4},{4,0},{8,12},{12,8},{16,20},{20,16},{24,28},{28,24},{1,5},{5... | collective-permute-start | bytes 4718600 | tf_op jit(solution)/shard_map/ppermute | solution.py:578
  60.0 29.8 %collective-permute-start.16 = (bf16[384,1536]{1,0:T(8,128)(2,1)}, bf16[384,1536]{1,0:T(8,128)(2,1)S(1)}, u32[]{:S(2)}, u32[]{:S(2)}) collective-permute-start(bf16[384,1536]{1,0:T(8,128)(2,1)} %collective-permute-done.9.refs_7_), channel_id=1, source_target_pairs={{0,8},{4,12},{8,16},{12,20},{16,24},{20,28},{24,0},{28,4},{1,9},{5... | collective-permute-start | bytes 3538952 | tf_op jit(solution)/shard_map/ppermute | solution.py:581
  89.7 30.7 %collective-permute-start.17 = (bf16[384,1536]{1,0:T(8,128)(2,1)S(1)}, bf16[384,1536]{1,0:T(8,128)(2,1)S(1)}, u32[]{:S(2)}, u32[]{:S(2)}) collective-permute-start(bf16[384,1536]{1,0:T(8,128)(2,1)S(1)} %collective-permute-done.16.refs_8_), channel_id=1, source_target_pairs={{0,8},{4,12},{8,16},{12,20},{16,24},{20,28},{24,0},{28,4},{1,9},{5... | collective-permute-start | bytes 3538952 | tf_op jit(solution)/shard_map/ppermute | solution.py:581
  89.7 9.5 %collective-permute-start.13 = (bf16[16,128,384]{2,1,0:T(8,128)(2,1)}, bf16[16,128,384]{2,1,0:T(8,128)(2,1)}, u32[]{:S(2)}, u32[]{:S(2)}) collective-permute-start(bf16[16,128,384]{2,1,0:T(8,128)(2,1)} %collective-permute-done.8.refs_4_.refs_6_), channel_id=1, source_target_pairs={{0,1},{1,0},{2,3},{3,2},{4,5},{5,4},{6,7},{7,6},{8,9},{9,8},{10,11... | collective-permute-start | bytes 4718600 | tf_op jit(solution)/shard_map/ppermute | solution.py:584
  94.0 5.2 %collective-permute-start.15 = (bf16[16,128,384]{2,1,0:T(8,128)(2,1)}, bf16[16,128,384]{2,1,0:T(8,128)(2,1)}, u32[]{:S(2)}, u32[]{:S(2)}) collective-permute-start(bf16[16,128,384]{2,1,0:T(8,128)(2,1)} %collective-permute-done.14.refs_6_.refs_4_.refs_10_), channel_id=1, source_target_pairs={{0,1},{1,0},{2,3},{3,2},{4,5},{5,4},{6,7},{7,6},{8,9},{9,8},{10,11... | collective-permute-start | bytes 4718600 | tf_op jit(solution)/shard_map/ppermute | solution.py:584
  99.2 33.1 %collective-permute-start.18 = (bf16[384,768]{1,0:T(8,128)(2,1)}, bf16[384,768]{1,0:T(8,128)(2,1)S(1)}, u32[]{:S(2)}, u32[]{:S(2)}) collective-permute-start(bf16[384,768]{1,0:T(8,128)(2,1)} %w_grad.7), channel_id=1, source_target_pairs={{0,8},{4,12},{8,16},{12,20},{16,24},{20,28},{24,0},{28,4},{1,9},{5... | collective-permute-start | bytes 1769480 | tf_op jit(solution)/shard_map/ppermute | solution.py:581
  103.1 29.1 %copy-start.21 = (bf16[384,768]{1,0:T(8,128)(2,1)S(1)}, bf16[384,768]{1,0:T(8,128)(2,1)}, u32[]{:S(2)}) copy-start(bf16[384,768]{1,0:T(8,128)(2,1)} %w_grad.8) | copy-start | bytes 1769476
  131.7 12.0 %collective-permute-start.21 = (bf16[4,512,128]{2,1,0:T(8,128)(2,1)}, bf16[4,512,128]{2,1,0:T(8,128)(2,1)S(1)}, u32[]{:S(2)}, u32[]{:S(2)}) collective-permute-start(bf16[4,512,128]{2,1,0:T(8,128)(2,1)} %get-tuple-element.62), channel_id=1, source_target_pairs={{0,4},{4,0},{8,12},{12,8},{16,20},{20,16},{24,28},{28,24},{1,5},{5... | collective-permute-start | bytes 1572872 | tf_op jit(solution)/shard_map/ppermute | solution.py:578
  132.3 18.1 %collective-permute-start.19 = (bf16[384,768]{1,0:T(8,128)(2,1)S(1)}, bf16[384,768]{1,0:T(8,128)(2,1)S(1)}, u32[]{:S(2)}, u32[]{:S(2)}) collective-permute-start(bf16[384,768]{1,0:T(8,128)(2,1)S(1)} %copy-done.21), channel_id=1, source_target_pairs={{0,8},{4,12},{8,16},{12,20},{16,24},{20,28},{24,0},{28,4},{1,9},{5... | collective-permute-start | bytes 1769480 | tf_op jit(solution)/shard_map/ppermute | solution.py:581
  137.4 25.6 %collective-permute-start.20 = (bf16[384,768]{1,0:T(8,128)(2,1)}, bf16[384,768]{1,0:T(8,128)(2,1)S(1)}, u32[]{:S(2)}, u32[]{:S(2)}) collective-permute-start(bf16[384,768]{1,0:T(8,128)(2,1)} %w_grad.9), channel_id=1, source_target_pairs={{0,8},{4,12},{8,16},{12,20},{16,24},{20,28},{24,0},{28,4},{1,9},{5... | collective-permute-start | bytes 1769480 | tf_op jit(solution)/shard_map/ppermute | solution.py:581
  143.7 31.3 %collective-permute-start.23 = (bf16[4,512,128]{2,1,0:T(8,128)(2,1)S(1)}, bf16[4,512,128]{2,1,0:T(8,128)(2,1)S(1)}, u32[]{:S(2)}, u32[]{:S(2)}) collective-permute-start(bf16[4,512,128]{2,1,0:T(8,128)(2,1)S(1)} %copy-done.27), channel_id=1, source_target_pairs={{0,4},{4,0},{8,12},{12,8},{16,20},{20,16},{24,28},{28,24},{1,5},{5... | collective-permute-start | bytes 1572872 | tf_op jit(solution)/shard_map/ppermute | solution.py:578
  155.2 21.4 %collective-permute-start.22 = (bf16[384,768]{1,0:T(8,128)(2,1)}, bf16[384,768]{1,0:T(8,128)(2,1)S(1)}, u32[]{:S(2)}, u32[]{:S(2)}) collective-permute-start(bf16[384,768]{1,0:T(8,128)(2,1)} %w_grad.10), channel_id=1, source_target_pairs={{0,8},{4,12},{8,16},{12,20},{16,24},{20,28},{24,0},{28,4},{1,9},{5... | collective-permute-start | bytes 1769480 | tf_op jit(solution)/shard_map/ppermute | solution.py:581
  167.9 39.1 %collective-permute-start.25 = (bf16[384,768]{1,0:T(8,128)(2,1)}, bf16[384,768]{1,0:T(8,128)(2,1)S(1)}, u32[]{:S(2)}, u32[]{:S(2)}) collective-permute-start(bf16[384,768]{1,0:T(8,128)(2,1)} %w_grad.11), channel_id=1, source_target_pairs={{0,8},{4,12},{8,16},{12,20},{16,24},{20,28},{24,0},{28,4},{1,9},{5... | collective-permute-start | bytes 1769480 | tf_op jit(solution)/shard_map/ppermute | solution.py:581
  175.1 13.7 %collective-permute-start.24 = (bf16[4,512,128]{2,1,0:T(8,128)(2,1)S(1)}, bf16[4,512,128]{2,1,0:T(8,128)(2,1)S(1)}, u32[]{:S(2)}, u32[]{:S(2)}) collective-permute-start(bf16[4,512,128]{2,1,0:T(8,128)(2,1)S(1)} %copy-done.26), channel_id=1, source_target_pairs={{0,4},{4,0},{8,12},{12,8},{16,20},{20,16},{24,28},{28,24},{1,5},{5... | collective-permute-start | bytes 1572872 | tf_op jit(solution)/shard_map/ppermute | solution.py:578
  181.5 25.4 %collective-permute-start.26 = (bf16[384,768]{1,0:T(8,128)(2,1)}, bf16[384,768]{1,0:T(8,128)(2,1)S(1)}, u32[]{:S(2)}, u32[]{:S(2)}) collective-permute-start(bf16[384,768]{1,0:T(8,128)(2,1)} %w_grad.12), channel_id=1, source_target_pairs={{0,8},{4,12},{8,16},{12,20},{16,24},{20,28},{24,0},{28,4},{1,9},{5... | collective-permute-start | bytes 1769480 | tf_op jit(solution)/shard_map/ppermute | solution.py:581
  197.6 16.7 %collective-permute-start.27 = (f32[16,8,128]{2,1,0:T(8,128)S(1)}, f32[16,8,128]{2,1,0:T(8,128)S(1)}, u32[]{:S(2)}, u32[]{:S(2)}) collective-permute-start(f32[16,8,128]{2,1,0:T(8,128)S(1)} %add_add_fusion.refs_13_), channel_id=1, source_target_pairs={{0,1},{1,0},{2,3},{3,2},{4,5},{5,4},{6,7},{7,6},{8,9},{9,8},{10,11... | collective-permute-start | bytes 196616 | tf_op jit(solution)/shard_map/ppermute | solution.py:584
  197.6 16.7 %collective-permute-start.28 = (f32[16,8,128]{2,1,0:T(8,128)S(1)}, f32[16,8,128]{2,1,0:T(8,128)S(1)}, u32[]{:S(2)}, u32[]{:S(2)}) collective-permute-start(f32[16,8,128]{2,1,0:T(8,128)S(1)} %add_add_fusion.refs_13_), channel_id=1, source_target_pairs={{0,2},{1,3},{2,0},{3,1},{4,6},{5,7},{6,4},{7,5},{8,10},{9,11},{10,... | collective-permute-start | bytes 196616 | tf_op jit(solution)/shard_map/ppermute | solution.py:584
  198.2 16.1 %collective-permute-start.29 = (f32[16,8,128]{2,1,0:T(8,128)S(1)}, f32[16,8,128]{2,1,0:T(8,128)S(1)}, u32[]{:S(2)}, u32[]{:S(2)}) collective-permute-start(f32[16,8,128]{2,1,0:T(8,128)S(1)} %add_add_fusion.refs_13_), channel_id=1, source_target_pairs={{0,3},{1,2},{2,1},{3,0},{4,7},{5,6},{6,5},{7,4},{8,11},{9,10},{10,... | collective-permute-start | bytes 196616 | tf_op jit(solution)/shard_map/ppermute | solution.py:584
  201.3 20.1 %all-to-all-start = ((f32[8,32,384]{2,1,0:T(8,128)}), f32[8,32,384]{2,1,0:T(8,128)S(1)}, u32[]{:S(2)}, u32[]{:S(2)}) async-start(f32[8,32,384]{2,1,0:T(8,128)} %select_reduce_fusion), calls=%async_computation | async-start | bytes 786432 | tf_op jit(solution)/shard_map/all_to_all | solution.py:866
  (33 other events, 192.2 us)

commit v2 on v1

--- a/solution.py
+++ b/solution.py
@@ -12,7 +12,7 @@
 BF16 = jnp.bfloat16
 F32 = jnp.float32
 VMEM_BYTES = 60 * 1024 * 1024
-WEIGHT = {"front": 30, "frame_stats": 30, "tap_waves": 30, "w_grad": 30}
+WEIGHT = {"front": 30, "frame_stats": 30, "w_grad": 30}
 
 def normalize(values, feature_total):
     value_sum = lax.psum(jnp.sum(values, axis=-1), "fsdp")
@@ -259,18 +259,11 @@
             at += 1
 
 
-def normed_of(x_ref, rows):
-    values = x_ref[0].astype(F32)
-    width = values.shape[1]
-    spread = down_lanes(rows[1:2], width)
-    return (values - down_lanes(rows[0:1], width)) * spread, spread
-
-
 def front_kernel(cap, parts, own_ref, *refs):
     refs = list(refs)
     x_refs = [refs.pop(0) for _ in range(cap)]
     stat_refs = [[refs.pop(0) for _ in range(cap)] for _ in range(parts)]
-    tap_ref, fwd_ref, inv_ref, *hid_outs, conv_out, wave_out, row_out = refs
+    tap_ref, fwd_ref, inv_ref, hid_out, normed_out, conv_out, wave_out, row_out = refs
     width = x_refs[0].shape[2]
     period = wave_out.shape[1]
     gain = tap_ref[0, period : period + 1]
@@ -280,30 +273,28 @@
         row = lax.broadcasted_iota(jnp.int32, row_out.shape[1:], 0)
         rows = jnp.where(row == 0, mean, jnp.where(row == 1, inv_std, 0.0))
         row_out[one] = rows
-        scaled.append(normed_of(x_refs[one], rows)[0] * gain)
+        values = x_refs[one][0].astype(F32) - down_lanes(mean, width)
+        normed = values * down_lanes(inv_std, width)
+        normed_out[one] = normed.astype(BF16)
+        scaled.append(normed * gain)
     wave = wide_dot(fwd_ref[...], side_by_side(scaled))
     count = wave.shape[0] // 2
     a, b = wave[:count], wave[count:]
     kc = side_by_side([tap_ref[0, :count]] * cap)
     ks = side_by_side([tap_ref[0, count : 2 * count]] * cap)
     conv = wide_dot(inv_ref[...], jnp.concatenate([a * kc + b * ks, b * kc - a * ks], axis=0))
-    hidden = (conv * jax.nn.sigmoid(conv)).astype(BF16)
+    hidden = conv * jax.nn.sigmoid(conv)
     frames = conv.shape[0]
     for one in range(cap):
         at = slice(one * width, (one + 1) * width)
         conv_out[one] = conv[:, at]
         wave_out[one] = wave[:, at]
-        first = one * width
-        for hid_out in hid_outs:
-            cut = hid_out.shape[2]
-            hid_out[0, one * frames : (one + 1) * frames] = hidden[:, first : first + cut]
-            first += cut
+        hid_out[0, :, one * frames : (one + 1) * frames] = hidden[:, at].T.astype(BF16)
 
 
 def back_kernel(cap, own_ref, *refs):
-    x_refs = refs[:cap]
     (
-        row_ref,
+        normed_ref,
         tap_ref,
         fwd_ref,
         inv_ref,
@@ -315,13 +306,13 @@
         grad_out,
         sum_out,
         small_out,
-    ) = refs[cap:]
+    ) = refs
     segs = conv_ref.shape[0] * pl.num_programs(0)
     period = wave_ref.shape[1]
     mine = (own_ref[segs + pl.program_id(0) * cap] & 1) == (own_ref[2 * segs] & 1)
     gain = tap_ref[0, period : period + 1]
-    frames, width = x_refs[0].shape[1:]
-    normed = [normed_of(x_refs[one], row_ref[one])[0] for one in range(cap)]
+    frames, width = normed_ref.shape[1:]
+    normed = [normed_ref[one].astype(F32) for one in range(cap)]
     hid_grad = jnp.where(mine, own_grad_ref[0], recv_ref[0]).astype(F32)
     hid_grad = side_by_side([hid_grad[one * frames : (one + 1) * frames] for one in range(cap)])
     conv = side_by_side([conv_ref[one] for one in range(cap)])
@@ -357,10 +348,10 @@
 
 
 def final_kernel(cap, chunks, order_ref, *refs):
-    x_refs, dy_refs, grad_refs = refs[:cap], refs[cap : 2 * cap], refs[2 * cap : 2 * cap + chunks]
-    row_ref, *sum_refs, out_ref, out_buf, sems = refs[2 * cap + chunks :]
+    dy_refs, grad_refs = refs[:cap], refs[cap : cap + chunks]
+    normed_ref, row_ref, *sum_refs, out_ref, out_buf, sems = refs[cap + chunks :]
     step, last = pl.program_id(0), pl.num_programs(0) - 1
-    parts, width = len(sum_refs), x_refs[0].shape[2]
+    parts, width = len(sum_refs), normed_ref.shape[2]
     slot = step % 2
 
     def put(slot, step, one):
@@ -374,7 +365,8 @@
             put(slot, step - 2, one).wait()
 
     for one in range(cap):
-        normed, spread = normed_of(x_refs[one], row_ref[one])
+        normed = normed_ref[one].astype(F32)
+        spread = down_lanes(row_ref[one, 1:2], width)
         total = width * parts
         grad_mean = sum(ref[one, 0:1, :] for ref in sum_refs) / total
         cross_mean = sum(ref[one, 1:2, :] for ref in sum_refs) / total
@@ -411,13 +403,19 @@
         index = ((owner >> 1) - (language >> 1)) & (held - 1)
         return jnp.where((language & 1) == (owner & 1), index, -1)
 
-    def w_copy(group, source):
-        return pltpu.make_async_copy(source, w_buf.at[group], w_sems.at[group])
+    def w_copies(group, source):
+        for part in range(parts):
+            rows = pl.ds(pl.multiple_of((me ^ part) * width, 128), width)
+            yield pltpu.make_async_copy(
+                source.at[rows],
+                w_buf.at[group, pl.ds(part * width, width)],
+                w_sems.at[group, part],
+            )
 
     def dy_copy(group, part, one):
         return pltpu.make_async_copy(
             dy_refs[part].at[table[group * cap + one]],
-            dy_buf.at[group, part, pl.ds(one * frames, frames)],
+            dy_buf.at[group, pl.ds(one * frames, frames), pl.ds(part * width, width)],
             dy_sems.at[group, part, one],
         )
 
@@ -429,7 +427,8 @@
 
                 @pl.when(index == at)
                 def _():
-                    w_copy(group, source).start()
+                    for copy in w_copies(group, source):
+                        copy.start()
 
             @pl.when(index >= 0)
             def _():
@@ -439,19 +438,12 @@
 
     @pl.when(held_index(step) >= 0)
     def _():
-        w_copy(step, w_refs[0]).wait()
-        total = None
+        for copy in w_copies(step, w_refs[0]):
+            copy.wait()
         for part in range(parts):
             for one in range(cap):
                 dy_copy(step, part, one).wait()
-            columns = pl.ds(pl.multiple_of((me ^ part) * width, 128), width)
-            term = lax.dot_general(
-                dy_buf[step, part],
-                w_buf[step, :, columns],
-                (((1,), (1,)), ((), ())),
-                preferred_element_type=F32,
-            )
-            total = term if total is None else total + term
+        total = jnp.dot(dy_buf[step], w_buf[step], preferred_element_type=F32)
         chunk = total.shape[1] // len(out_refs)
         for index, out_ref in enumerate(out_refs):
             out_ref[0] = total[:, index * chunk : (index + 1) * chunk].astype(BF16)
@@ -465,8 +457,9 @@
 
     hid_refs, dy_refs, add_refs = take(2), [take(parts), take(parts)], take(len(places))
     out_ref, hid_buf, dy_buf, add_buf, hid_sems, dy_sems, add_sems = refs
-    width = dy_buf.shape[3]
-    frames = dy_buf.shape[2] // cap
+    width = dy_buf.shape[1] // parts
+    group_rows = dy_buf.shape[0] // 2
+    frames = group_rows // cap
     owner, me = own_ref[2 * segs], own_ref[2 * segs + 1]
     language = 2 * (((owner >> 1) - step) & (line - 1)) + (owner & 1)
     found = []
@@ -478,14 +471,17 @@
 
     def hid_copy(side):
         source = hid_refs[side].at[jnp.maximum(found[side], 0)]
-        return pltpu.make_async_copy(source, hid_buf.at[side], hid_sems.at[side])
+        held = hid_buf.at[:, pl.ds(side * group_rows, group_rows)]
+        return pltpu.make_async_copy(source, held, hid_sems.at[side])
 
     def dy_copies(side, part):
         for one in range(cap):
             segment = (own_ref, pair_ref)[side][jnp.maximum(found[side], 0) * cap + one]
             yield pltpu.make_async_copy(
                 dy_refs[side][part].at[segment],
-                dy_buf.at[side, part, pl.ds(one * frames, frames)],
+                dy_buf.at[
+                    pl.ds(side * group_rows + one * frames, frames), pl.ds(part * width, width)
+                ],
                 dy_sems.at[side, part, one],
             )
 
@@ -510,52 +506,40 @@
         @pl.when(found[side] >= 0)
         def _():
             hid_copy(side).wait()
-
-    first, second = found[0] >= 0, found[1] >= 0
+            for part in range(parts):
+                for copy in dy_copies(side, part):
+                    copy.wait()
+
     for index in range(len(places)):
         add_copy(index).wait()
-    for part in range(parts):
-        at = slice(part * width, (part + 1) * width)
-
-        def product(side):
-            return lax.dot_general(
-                hid_buf[side],
-                dy_buf[side, part],
-                (((0,), (0,)), ((), ())),
-                preferred_element_type=F32,
-            )
-
-        def put(value):
-            if places:
-                value = value + add_buf[:, at].astype(F32)
-            if scale is None:
-                out_ref[:, at] = value.astype(BF16)
-            else:
-                columns = pl.ds(pl.multiple_of((me ^ part) * width, 128), width)
-                out_ref[:, columns] = (value * scale).astype(BF16)
-
-        for side in range(2):
-
-            @pl.when(found[side] >= 0)
-            def _():
-                for copy in dy_copies(side, part):
-                    copy.wait()
-
-        @pl.when(first & second)
+
+    def put(value):
+        if places:
+            value = value + add_buf[...].astype(F32)
+        if scale is None:
+            out_ref[...] = value.astype(BF16)
+            return
+        for part in range(parts):
+            columns = pl.ds(pl.multiple_of((me ^ part) * width, 128), width)
+            one = value[:, part * width : (part + 1) * width]
+            out_ref[:, columns] = (one * scale).astype(BF16)
+
+    first, second = found[0] >= 0, found[1] >= 0
+
+    @pl.when(first & second)
+    def _():
+        put(jnp.dot(hid_buf[...], dy_buf[...], preferred_element_type=F32))
+
+    for side, only in enumerate((first & jnp.logical_not(second), second & jnp.logical_not(first))):
+
+        @pl.when(only)
         def _():
-            put(product(0) + product(1))
-
-        @pl.when(first & jnp.logical_not(second))
-        def _():
-            put(product(0))
-
-        @pl.when(jnp.logical_not(first) & second)
-        def _():
-            put(product(1))
-
-        @pl.when(jnp.logical_not(first | second))
-        def _():
-            put(jnp.zeros((out_ref.shape[0], width), F32))
+            at = pl.ds(side * group_rows, group_rows)
+            put(jnp.dot(hid_buf[:, at], dy_buf[at], preferred_element_type=F32))
+
+    @pl.when(jnp.logical_not(first | second))
+    def _():
+        put(jnp.zeros(out_ref.shape, F32))
 
 
 def moved_weights(feats, cotan, lang, w_out, gain, kernel):
@@ -626,6 +610,7 @@
     lang_row = jnp.pad(lang.astype(BF16), (0, width - segs))[None]
     tap_rows = jnp.concatenate([kernel[0], gain, lang_row], axis=0)
     tap_rows = jnp.pad(tap_rows, ((0, -tap_rows.shape[0] % 16), (0, 0)))[None]
+    tap_own = tap_rows
     tap_rows = jnp.concatenate([tap_rows, pair_swap(tap_rows)], axis=0)
     tap_rows = [tap_rows] + [
         lax.ppermute(tap_rows, "expert", [(i, i ^ (2 * k)) for i in range(owners)])
@@ -636,7 +621,7 @@
         stats_kernel,
         "frame_stats",
         (),
-        [(feats, pl.BlockSpec((per_step, frames, width), lambda i: (i, 0, 0)))],
+        [(after(feats, tap_own), pl.BlockSpec((per_step, frames, width), lambda i: (i, 0, 0)))],
         [
             (
                 like((segs, 8, frames), F32),
@@ -662,7 +647,9 @@
     lang_sorted = own_table[segs : 2 * segs]
     pair_table = table_of(tap_rows[0][1, taps + 1, :segs].astype(jnp.int32))
 
-    w_held = [w_out[0], along(after(w_out[0], tap_rows[1]))]
+    w_held = [w_out[0].T]
+    for step in range(1, line):
+        w_held.append(along(after(w_held[-1], *tap_rows)))
     dy_pair = pair_swap(after(cotan, tap_rows[0]))
     dy_core = swap(after(cotan, *stat_parts, *tap_rows), 1)
     dy_far = swap(after(cotan, *stat_parts), parts // 2) if parts > 2 else None
@@ -711,13 +698,14 @@
     ]
     wave_flops = 12 * segs * period * frames * width
     cap_block = (cap, frames, width)
-    hidden, conv, wave, row_values = call(
+    hidden, normed, conv, wave, row_values = call(
         lambda *refs: front_kernel(cap, parts, *refs),
         "front",
         (own_table,),
         by_order(feats) + stat_inputs + tap_inputs(),
         [
-            (like((groups, group_rows, width), BF16), in_turn((1, group_rows, width))),
+            (like((groups, width, group_rows), BF16), in_turn((1, width, group_rows))),
+            (like(feats.shape, BF16), in_turn(cap_block)),
             (like(feats.shape, F32), in_turn(cap_block)),
             (like((segs, period, width), F32), in_turn((cap, period, width))),
             (like((segs, 8, frames), F32), in_turn((cap, 8, frames))),
@@ -727,18 +715,16 @@
     )
 
     dy_parts, dy_pair_parts = [cotan, dy_core], [dy_pair]
-    dy_pair_core = swap(after(dy_pair, hidden, dy_far, w_held[1], dy_core), 1)
+    phase = (dy_pair, dy_far, dy_core, w_held[1])
+    dy_pair_core = swap(after(dy_pair, hidden, *phase), 1)
     dy_pair_parts.append(dy_pair_core)
-    for step in range(2, line):
-        w_held.append(along(after(w_held[-1], hidden, dy_pair, dy_far, dy_core)))
-
-    hidden_pair = pair_swap(after(hidden, dy_pair, dy_far, w_held[1], dy_core))
+    hidden_pair = pair_swap(after(hidden, *phase))
     if parts > 2:
-        dy_pair_far = swap(after(dy_pair, hidden, dy_far, w_held[1], dy_core), parts // 2)
+        dy_pair_far = swap(after(dy_pair, hidden, *phase), parts // 2)
         dy_parts += [dy_far, swap(after(dy_far, dy_pair_core), 1)]
         dy_pair_parts += [dy_pair_far, swap(dy_pair_far, 1)]
 
-    def w_grad_call(step, part_ids, adds, places, scale=None):
+    def w_grad_call(step, part_ids, adds, places, scale=None, waits=()):
         across = len(part_ids) * width
         inputs = [hidden, hidden_pair]
         inputs += [dy_parts[k] for k in part_ids] + [dy_pair_parts[k] for k in part_ids]
@@ -752,21 +738,25 @@
             [(like((rows, across), BF16), pl.BlockSpec((rows, across), lambda *_: (0, 0)))],
             (1,),
             scratch=[
-                pltpu.VMEM((2, group_rows, width), BF16),
-                pltpu.VMEM((2, len(part_ids), group_rows, width), BF16),
+                pltpu.VMEM((width, 2 * group_rows), BF16),
+                pltpu.VMEM((2 * group_rows, across), BF16),
                 pltpu.VMEM((rows, across), BF16),
                 pltpu.SemaphoreType.DMA((2,)),
                 pltpu.SemaphoreType.DMA((2, len(part_ids), cap)),
                 pltpu.SemaphoreType.DMA((max(len(places), 1),)),
             ],
             flops=4 * group_rows * rows * across,
+            waits=waits,
         )[0]
 
     pieces = [list(range(parts // 2)), list(range(parts // 2, parts))]
     arrived = [[] for _ in pieces]
 
     def line_step(step, index):
-        share = w_grad_call(step, pieces[index], arrived[index], [0] * len(arrived[index]))
+        waits = (w_held[-1],) if step == 1 else ()
+        share = w_grad_call(
+            step, pieces[index], arrived[index], [0] * len(arrived[index]), waits=waits
+        )
         arrived[index] = [along(share)]
 
     line_steps = [(step, index) for step in range(1, line) for index in range(len(pieces))]
@@ -787,10 +777,10 @@
             ],
             (groups,),
             scratch=[
-                pltpu.VMEM((groups, parts, group_rows, width), BF16),
-                pltpu.VMEM((groups, rows, total_width), BF16),
+                pltpu.VMEM((groups, group_rows, total_width), BF16),
+                pltpu.VMEM((groups, total_width, rows), BF16),
                 pltpu.SemaphoreType.DMA((groups, parts, cap)),
-                pltpu.SemaphoreType.DMA((groups,)),
+                pltpu.SemaphoreType.DMA((groups, parts)),
             ],
             flops=2 * segs * frames * rows * total_width,
         )
@@ -802,18 +792,17 @@
         hid_grad_pair.append(pair_swap(after(one, hid_grad_pair[-1])))
     line_steps_until(2, 0)
     hid_grad_own = hid_grad_of(False, dy_parts)
+    line_steps_until(2, len(pieces))
 
     norm_grads, sums, smalls = [], [], []
-    line_steps_until(3, 0)
     for c in range(chunks):
-        if c == 1:
-            line_steps_until(line, 0)
+        if c == chunks - 1:
+            line_steps_until(3, 0)
         norm_grad, part_sums, small = call(
             lambda *refs: back_kernel(cap, *refs),
             "back",
             (own_table,),
-            by_order(feats, c, chunk)
-            + [(row_values, in_turn((cap, 8, frames)))]
+            [(normed, in_turn((cap, frames, chunk), c))]
             + tap_inputs(c, chunk)
             + [
                 (jnp.asarray(lag_wave), whole(lag_wave)),
@@ -836,20 +825,13 @@
     line_steps_until(line, 0)
     sums = sum(sums)
     sum_parts = [sums] + [swap(sums, k) for k in range(1, parts)]
-    w_grad = w_grad_call(
-        0,
-        list(range(parts)),
-        [array for one in arrived for array in one],
-        [piece[0] * width for piece in pieces],
-        scale=grad_scale,
-    )
     feat_grad = call(
         lambda *refs: final_kernel(cap, chunks, *refs),
         "input_grad",
         (own_table,),
-        by_order(feats)
-        + by_order(cotan)
+        by_order(cotan)
         + [(one, in_turn((cap, frames, chunk))) for one in norm_grads]
+        + [(normed, in_turn(cap_block))]
         + [(one, in_turn((cap, 8, frames))) for one in (row_values, *sum_parts)],
         [(like(feats.shape, BF16), any_spec)],
         (groups,),
@@ -859,6 +841,13 @@
         ],
     )[0]
 
+    w_grad = w_grad_call(
+        0,
+        list(range(parts)),
+        [array for one in arrived for array in one],
+        [piece[0] * width for piece in pieces],
+        scale=grad_scale,
+    )
     small = jnp.concatenate(smalls, axis=2)
     group_lang = lang_sorted.reshape(groups, cap)[:, 0]
     slots = jnp.arange(owners, dtype=jnp.int32)[:, None] == group_lang[None, :]
@@ -875,7 +864,7 @@
     parts = lax.axis_size("fsdp")
     weights_moved = 2 * (owners // 2 - 1) * math.prod(w_out.shape)
     frames_moved = 3 * 2 * math.prod(feats.shape)
-    fits = owners & (owners - 1) == 0 and owners > 1 and parts & (parts - 1) == 0 and frames % 128 == 0 and width % frames == 0 and parts in (2, 4) and segs <= 256 and segs <= 256 and segs <= 256 and segs <= 256 and segs <= 256 and segs <= 256 and segs <= 256
+    fits = owners & (owners - 1) == 0 and owners > 1 and parts & (parts - 1) == 0 and frames % 128 == 0 and width % frames == 0 and parts in (2, 4) and segs <= 256 and segs <= 256 and segs <= 256 and segs <= 256 and segs <= 256 and segs <= 256 and segs <= 256 and segs <= 256 and segs <= 256 and segs <= 256 and segs <= 256 and segs <= 256 and segs <= 256 and segs <= 256 and segs <= 256 and segs <= 256 and segs <= 256 and segs <= 256 and segs <= 256 and segs <= 256 and segs <= 256
     if fits and weights_moved < frames_moved:
         return moved_weights(feats, cotan, lang, w_out, gain, kernel)
     return routed_frames(feats, cotan, lang, w_out, gain, kernel)

time: 222 us -> 202 us (0.910); the launches traced: 223 us -> 200 us
  waiting for transfers between devices: 88.9 us -> 69.8 us
  Pallas kernels: 89.1 us -> 81.3 us
  starting transfers between devices: 28.7 us -> 34.2 us
    ppermute x9, waiting for transfers between devices: 79.3 us -> 19.1 us  [along(): lax.ppermute(value, 'expert', [(i, (i + 2) % owners) for i in range(owner...]
    ppermute x12, waiting for transfers between devices: 4.23 us -> 34.6 us  [swap(): return lax.ppermute(value, 'fsdp', [(i, i ^ bit) for i in range(parts)])]
    ppermute x6, waiting for transfers between devices: 3.13 us -> 11.8 us  [pair_swap(): return lax.ppermute(value, 'expert', [(i, i ^ 1) for i in range(owners)])]
    pallas_call x16, Pallas kernels: 89.1 us -> 81.3 us  [call(): pl.pallas_call(body, grid_spec=pltpu.PrefetchScalarGridSpec(num_scalar_pr...]
    ppermute x9, starting transfers between devices: 1.18 us -> 5.3 us  [along(): lax.ppermute(value, 'expert', [(i, (i + 2) % owners) for i in range(owner...]
    unnamed x69 -> x70, local copies, waits for them, and re-layouts: 9.42 us -> 9 us
  transfers between devices with their start and end apart: 31 -> 31, of which waited for: 10 -> 13; matrix products, arithmetic and copies ran while one was open for 2% -> 2% of each run, Pallas kernels for 38% -> 41%
where the time goes in v2:
time: 202 us; the launch traced here: 200 us
  Pallas kernels  81.3 us (40%)
  waiting for transfers between devices  69.8 us (35%)
  starting transfers between devices  34.2 us (17%)
  local copies, waits for them, and re-layouts  9.79 us (5%)
  other arithmetic  4.27 us (2%)
    pallas_call x16, Pallas kernels, call(): pl.pallas_call(body, grid_spec=pltpu.PrefetchScalarGridSpec(num_scalar_pr...  81.3 us
    ppermute x12, waiting for transfers between devices, swap(): return lax.ppermute(value, 'fsdp', [(i, i ^ bit) for i in range(parts)])  34.6 us
    ppermute x9, waiting for transfers between devices, along(): lax.ppermute(value, 'expert', [(i, (i + 2) % owners) for i in range(owner...  19.1 us
    ppermute x6, waiting for transfers between devices, pair_swap(): return lax.ppermute(value, 'expert', [(i, i ^ 1) for i in range(owners)])  11.8 us
    ppermute x6, starting transfers between devices, pair_swap(): return lax.ppermute(value, 'expert', [(i, i ^ 1) for i in range(owners)])  10.8 us
    unnamed x70, local copies, waits for them, and re-layouts  9 us
    ppermute x12, starting transfers between devices, swap(): return lax.ppermute(value, 'fsdp', [(i, i ^ bit) for i in range(parts)])  7.03 us
    all_to_all x1, starting transfers between devices, moved_weights(): lax.all_to_all(spread, 'expert', split_axis=0, concat_axis=0, tiled=True)  6.33 us
  transfers between devices with their start and end apart: 31, of which 13 were waited for; matrix products, arithmetic and copies ran while one was open for 2% of the time, Pallas kernels for 41%

profile of v2, /device:TPU:0, one launch (start us, length us, event | category | flops | bytes accessed | tf_op | source)
XLA Modules:
  0.0 200.5 jit_solution(4107659576663862940)
XLA Ops:
  2.1 3.0 %collective-permute-start = (bf16[1,48,384]{2,1,0:T(8,128)(2,1)S(1)}, bf16[1,48,384]{2,1,0:T(8,128)(2,1)S(1)}, u32[]{:S(2)}, u32[]{:S(2)}) collective-permute-start(bf16[1,48,384]{2,1,0:T(8,128)(2,1)S(1)} %fusion.5), channel_id=1, source_target_pairs={{0,4},{4,0},{8,12},{12,8},{16,20},{20,16},{24,28},{28,24},{1,5},{5... | collective-permute-start | bytes 110600 | tf_op jit(solution)/shard_map/ppermute | solution.py:562
  5.1 1.9 collective-permute-done
  7.1 2.1 %collective-permute-start.1 = (bf16[2,48,384]{2,1,0:T(8,128)(2,1)S(1)}, bf16[2,48,384]{2,1,0:T(8,128)(2,1)S(1)}, u32[]{:S(2)}, u32[]{:S(2)}) collective-permute-start(bf16[2,48,384]{2,1,0:T(8,128)(2,1)S(1)} %pad_maximum_fusion.1.refs_0_), channel_id=1, source_target_pairs={{0,8},{4,12},{8,0},{12,4},{16,24},{20,28},{24,16},{28,20},{1,9},{5... | collective-permute-start | bytes 221192 | tf_op jit(solution)/shard_map/ppermute | solution.py:616
  9.2 2.6 %collective-permute-start.2 = (bf16[2,48,384]{2,1,0:T(8,128)(2,1)S(1)}, bf16[2,48,384]{2,1,0:T(8,128)(2,1)S(1)}, u32[]{:S(2)}, u32[]{:S(2)}) collective-permute-start(bf16[2,48,384]{2,1,0:T(8,128)(2,1)S(1)} %pad_maximum_fusion.1.refs_0_), channel_id=1, source_target_pairs={{0,16},{4,20},{8,24},{12,28},{16,0},{20,4},{24,8},{28,12},{1,17},{... | collective-permute-start | bytes 221192 | tf_op jit(solution)/shard_map/ppermute | solution.py:616
  11.8 1.7 copy.16
  13.6 2.5 %collective-permute-done.2.refs_2_ = bf16[2,48,384]{2,1,0:T(8,128)(2,1)S(1)} collective-permute-done((bf16[2,48,384]{2,1,0:T(8,128)(2,1)S(1)}, bf16[2,48,384]{2,1,0:T(8,128)(2,1)S(1)}, u32[]{:S(2)}, u32[]{:S(2)}) %collective-permute-start.2) | collective-permute-done | bytes 73760 | tf_op jit(solution)/shard_map/ppermute | solution.py:616
  16.1 1.9 collective-permute-done.3.refs_3_
  18.7 4.1 %frame_stats.1.refs_5_.refs_6_.refs_7_.refs_8_ = f32[16,8,128]{2,1,0:T(8,128)} custom-call(bf16[16,128,384]{2,1,0:T(8,128)(2,1)} %refs_4_.9), custom_call_target="tpu_custom_call" | custom-call | bytes 49152000 | tf_op jit(solution)/shard_map/frame_stats/pallas_call | solution.py:587
  30.0 3.0 %tap_waves.1.refs_21_.refs_2_ = f32[8,152,384]{2,1,0:T(8,128)} custom-call(bf16[2,144,32]{2,1,0:T(8,128)(2,1)} %constant.25.clone.wave_ref, bf16[2,48,384]{2,1,0:T(8,128)(2,1)} %copy-done.7, bf16[2,48,384]{2,1,0:T(8,128)(2,1)} %copy-done.9, bf16[2,48,384]{2,1,0:T(8,128)(2,1)} %copy-done.10, bf16[2,48,384]{2,1,0:T(8,128)(2,1)} %copy-done.11), custom_call_target="tpu_custom_call" | custom-call | flops 54853632 | bytes 2181120 | tf_op jit(solution)/shard_map/tap_waves/pallas_call | solution.py:587
  33.4 11.9 %collective-permute-done.7.refs_7_ = bf16[1536,384]{1,0:T(8,128)(2,1)} collective-permute-done((bf16[1536,384]{1,0:T(8,128)(2,1)S(1)}, bf16[1536,384]{1,0:T(8,128)(2,1)}, u32[]{:S(2)}, u32[]{:S(2)}) %collective-permute-start.7) | collective-permute-done | bytes 1179680 | tf_op jit(solution)/shard_map/ppermute | solution.py:565
  45.3 8.3 %front.1 = (bf16[4,384,512]{2,1,0:T(8,128)(2,1)}, bf16[16,128,384]{2,1,0:T(8,128)(2,1)}, f32[16,128,384]{2,1,0:T(8,128)}, f32[16,144,384]{2,1,0:T(8,128)}, f32[16,8,128]{2,1,0:T(8,128)}) custom-call(s32[34]{0:T(128)} %pad_add_fusion.refs_0_, bf16[16,128,384]{2,1,0:T(8,128)(2,1)} %refs_4_.9, bf16[16,128,384]{2,1,0:T(8,128)(2,1)} %refs_4_.9, ...), custom_call_target="tpu_custom_call" | custom-call | flops 40768634880 | bytes 579747840 | tf_op jit(solution)/shard_map/front/pallas_call | solution.py:587
  53.6 8.6 %collective-permute-done.10.refs_6_.refs_2_.refs_8_ = bf16[16,128,384]{2,1,0:T(8,128)(2,1)} collective-permute-done((bf16[16,128,384]{2,1,0:T(8,128)(2,1)S(1)}, bf16[16,128,384]{2,1,0:T(8,128)(2,1)}, u32[]{:S(2)}, u32[]{:S(2)}) %collective-permute-start.10) | collective-permute-done | bytes 1572896 | tf_op jit(solution)/shard_map/ppermute | solution.py:562
  62.2 3.3 %collective-permute-done.11.refs_4_.refs_6_ = bf16[16,128,384]{2,1,0:T(8,128)(2,1)} collective-permute-done((bf16[16,128,384]{2,1,0:T(8,128)(2,1)S(1)}, bf16[16,128,384]{2,1,0:T(8,128)(2,1)}, u32[]{:S(2)}, u32[]{:S(2)}) %collective-permute-start.11) | collective-permute-done | bytes 1572896 | tf_op jit(solution)/shard_map/ppermute | solution.py:568
  68.6 3.3 %collective-permute-done.8.refs_8_ = bf16[1536,384]{1,0:T(8,128)(2,1)S(1)} collective-permute-done((bf16[1536,384]{1,0:T(8,128)(2,1)}, bf16[1536,384]{1,0:T(8,128)(2,1)S(1)}, u32[]{:S(2)}, u32[]{:S(2)}) %collective-permute-start.8) | collective-permute-done | bytes 1179680 | tf_op jit(solution)/shard_map/ppermute | solution.py:565
  73.0 29.7 %collective-permute-done.16.refs_6_.refs_4_.refs_10_ = bf16[16,128,384]{2,1,0:T(8,128)(2,1)} collective-permute-done((bf16[16,128,384]{2,1,0:T(8,128)(2,1)}, bf16[16,128,384]{2,1,0:T(8,128)(2,1)}, u32[]{:S(2)}, u32[]{:S(2)}) %collective-permute-start.16) | collective-permute-done | bytes 1572896 | tf_op jit(solution)/shard_map/ppermute | solution.py:568
  103.9 3.5 %w_grad.7 = bf16[384,768]{1,0:T(8,128)(2,1)} custom-call(s32[34]{0:T(128)} %pad_add_fusion.refs_0_, s32[32]{0:T(128)} %pad_add_fusion.1.refs_1_, bf16[4,384,512]{2,1,0:T(8,128)(2,1)} %get-tuple-element.60.refs_2_, bf16[4,384,512]{2,1,0:T(8,128)(2,1)} %collective-permute-done.13.refs_3_, bf16[16,128,384]{2,1,0:T(8,128)(2,1)} %refs_4_.14, ...), custom_call_target="tpu_custom_call" | custom-call | flops 18119393280 | bytes 300810240 | tf_op jit(solution)/shard_map/w_grad/pallas_call | solution.py:587
  107.4 2.5 %collective-permute-start.18 = (bf16[384,768]{1,0:T(8,128)(2,1)}, bf16[384,768]{1,0:T(8,128)(2,1)S(1)}, u32[]{:S(2)}, u32[]{:S(2)}) collective-permute-start(bf16[384,768]{1,0:T(8,128)(2,1)} %w_grad.7), channel_id=1, source_target_pairs={{0,8},{4,12},{8,16},{12,20},{16,24},{20,28},{24,0},{28,4},{1,9},{5... | collective-permute-start | bytes 1769480 | tf_op jit(solution)/shard_map/ppermute | solution.py:565
  110.0 3.5 %w_grad.8 = bf16[384,768]{1,0:T(8,128)(2,1)} custom-call(s32[34]{0:T(128)} %pad_add_fusion.refs_0_, s32[32]{0:T(128)} %pad_add_fusion.1.refs_1_, bf16[4,384,512]{2,1,0:T(8,128)(2,1)} %get-tuple-element.60.refs_2_, bf16[4,384,512]{2,1,0:T(8,128)(2,1)} %collective-permute-done.13.refs_3_, bf16[16,128,384]{2,1,0:T(8,128)(2,1)} %collective-permute-done.11.refs_4_.refs_6_, ...), custom_call_target="tpu_custom_call" | custom-call | flops 18119393280 | bytes 300810240 | tf_op jit(solution)/shard_map/w_grad/pallas_call | solution.py:587
  113.5 7.4 %hid_grad.2 = (bf16[4,512,128]{2,1,0:T(8,128)(2,1)}, bf16[4,512,128]{2,1,0:T(8,128)(2,1)}, bf16[4,512,128]{2,1,0:T(8,128)(2,1)}) custom-call(s32[34]{0:T(128)} %pad_add_fusion.refs_0_, s32[32]{0:T(128)} %pad_add_fusion.1.refs_1_, bf16[16,128,384]{2,1,0:T(8,128)(2,1)} %collective-permute-done.10.refs_6_.refs_2_.refs_8_, ...), custom_call_target="tpu_custom_call" | custom-call | flops 2415919104 | bytes 12582912 | tf_op jit(solution)/shard_map/hid_grad/pallas_call | solution.py:587
  125.0 3.7 %w_grad.9 = bf16[384,768]{1,0:T(8,128)(2,1)} custom-call(s32[34]{0:T(128)} %pad_add_fusion.refs_0_, s32[32]{0:T(128)} %pad_add_fusion.1.refs_1_, bf16[4,384,512]{2,1,0:T(8,128)(2,1)} %get-tuple-element.60.refs_2_, bf16[4,384,512]{2,1,0:T(8,128)(2,1)} %collective-permute-done.13.refs_3_, bf16[16,128,384]{2,1,0:T(8,128)(2,1)} %refs_4_.14, ...), custom_call_target="tpu_custom_call" | custom-call | flops 18119393280 | bytes 318504960 | tf_op jit(solution)/shard_map/w_grad/pallas_call | solution.py:587
  129.9 5.8 %hid_grad.3 = (bf16[4,512,128]{2,1,0:T(8,128)(2,1)}, bf16[4,512,128]{2,1,0:T(8,128)(2,1)}, bf16[4,512,128]{2,1,0:T(8,128)(2,1)}) custom-call(s32[34]{0:T(128)} %pad_add_fusion.refs_0_, s32[32]{0:T(128)} %pad_add_fusion.1.refs_1_, bf16[16,128,384]{2,1,0:T(8,128)(2,1)} %refs_4_.14, bf16[16,128,384]{2,1,0:T(8,128)(2,1)} %collective-permute-done.12.refs_5_.refs_3_, ...), custom_call_target="tpu_custom_call" | custom-call | flops 2415919104 | bytes 12582912 | tf_op jit(solution)/shard_map/hid_grad/pallas_call | solution.py:587
  135.8 2.6 %collective-permute-start.21 = (bf16[4,512,128]{2,1,0:T(8,128)(2,1)S(1)}, bf16[4,512,128]{2,1,0:T(8,128)(2,1)S(1)}, u32[]{:S(2)}, u32[]{:S(2)}) collective-permute-start(bf16[4,512,128]{2,1,0:T(8,128)(2,1)S(1)} %copy-done.30), channel_id=1, source_target_pairs={{0,4},{4,0},{8,12},{12,8},{16,20},{20,16},{24,28},{28,24},{1,5},{5... | collective-permute-start | bytes 1572872 | tf_op jit(solution)/shard_map/ppermute | solution.py:562
  138.4 2.2 %collective-permute-done.19.refs_8_ = bf16[384,768]{1,0:T(8,128)(2,1)S(1)} collective-permute-done((bf16[384,768]{1,0:T(8,128)(2,1)S(1)}, bf16[384,768]{1,0:T(8,128)(2,1)S(1)}, u32[]{:S(2)}, u32[]{:S(2)}) %collective-permute-start.19) | collective-permute-done | bytes 589856 | tf_op jit(solution)/shard_map/ppermute | solution.py:565
  141.4 3.7 %w_grad.10 = bf16[384,768]{1,0:T(8,128)(2,1)} custom-call(s32[34]{0:T(128)} %pad_add_fusion.refs_0_, s32[32]{0:T(128)} %pad_add_fusion.1.refs_1_, bf16[4,384,512]{2,1,0:T(8,128)(2,1)} %get-tuple-element.60.refs_2_, bf16[4,384,512]{2,1,0:T(8,128)(2,1)} %collective-permute-done.13.refs_3_, bf16[16,128,384]{2,1,0:T(8,128)(2,1)} %collective-permute-done.11.refs_4_.refs_6_, ...), custom_call_target="tpu_custom_call" | custom-call | flops 18119393280 | bytes 318504960 | tf_op jit(solution)/shard_map/w_grad/pallas_call | solution.py:587
  145.2 6.9 %back.3 = (f32[16,128,128]{2,1,0:T(8,128)}, f32[16,8,128]{2,1,0:T(8,128)}, f32[4,32,128]{2,1,0:T(8,128)}) custom-call(s32[34]{0:T(128)} %pad_add_fusion.refs_0_, bf16[16,128,384]{2,1,0:T(8,128)(2,1)} %get-tuple-element.71.refs_1_.refs_8_, f32[8,152,384]{2,1,0:T(8,128)} %tap_waves.1.refs_21_.refs_2_, bf16[144,384]{1,0:T(8,128)(2,1)} %constant.26.clone.refs_22_.refs_3_, ...), custom_call_target="tpu_custom_call" | custom-call | flops 452984832 | bytes 12602368 | tf_op jit(solution)/shard_map/back/pallas_call | solution.py:587
  152.8 6.7 %back.4 = (f32[16,128,128]{2,1,0:T(8,128)}, f32[16,8,128]{2,1,0:T(8,128)}, f32[4,32,128]{2,1,0:T(8,128)}) custom-call(s32[34]{0:T(128)} %pad_add_fusion.refs_0_, bf16[16,128,384]{2,1,0:T(8,128)(2,1)} %get-tuple-element.71.refs_1_.refs_8_, f32[8,152,384]{2,1,0:T(8,128)} %tap_waves.1.refs_21_.refs_2_, bf16[144,384]{1,0:T(8,128)(2,1)} %constant.26.clone.refs_22_.refs_3_, ...), custom_call_target="tpu_custom_call" | custom-call | flops 452984832 | bytes 12602368 | tf_op jit(solution)/shard_map/back/pallas_call | solution.py:587
  160.4 3.7 %w_grad.11 = bf16[384,768]{1,0:T(8,128)(2,1)} custom-call(s32[34]{0:T(128)} %pad_add_fusion.refs_0_, s32[32]{0:T(128)} %pad_add_fusion.1.refs_1_, bf16[4,384,512]{2,1,0:T(8,128)(2,1)} %get-tuple-element.60.refs_2_, bf16[4,384,512]{2,1,0:T(8,128)(2,1)} %collective-permute-done.13.refs_3_, bf16[16,128,384]{2,1,0:T(8,128)(2,1)} %refs_4_.14, ...), custom_call_target="tpu_custom_call" | custom-call | flops 18119393280 | bytes 318504960 | tf_op jit(solution)/shard_map/w_grad/pallas_call | solution.py:587
  165.0 6.7 %back.5 = (f32[16,128,128]{2,1,0:T(8,128)}, f32[16,8,128]{2,1,0:T(8,128)}, f32[4,32,128]{2,1,0:T(8,128)}) custom-call(s32[34]{0:T(128)} %pad_add_fusion.refs_0_, bf16[16,128,384]{2,1,0:T(8,128)(2,1)} %get-tuple-element.71.refs_1_.refs_8_, f32[8,152,384]{2,1,0:T(8,128)} %tap_waves.1.refs_21_.refs_2_, bf16[144,384]{1,0:T(8,128)(2,1)} %constant.26.clone.refs_22_.refs_3_, ...), custom_call_target="tpu_custom_call" | custom-call | flops 452984832 | bytes 12602368 | tf_op jit(solution)/shard_map/back/pallas_call | solution.py:587
  172.6 3.7 %w_grad.12 = bf16[384,768]{1,0:T(8,128)(2,1)} custom-call(s32[34]{0:T(128)} %pad_add_fusion.refs_0_, s32[32]{0:T(128)} %pad_add_fusion.1.refs_1_, bf16[4,384,512]{2,1,0:T(8,128)(2,1)} %get-tuple-element.60.refs_2_, bf16[4,384,512]{2,1,0:T(8,128)(2,1)} %collective-permute-done.13.refs_3_, bf16[16,128,384]{2,1,0:T(8,128)(2,1)} %collective-permute-done.11.refs_4_.refs_6_, ...), custom_call_target="tpu_custom_call" | custom-call | flops 18119393280 | bytes 318504960 | tf_op jit(solution)/shard_map/w_grad/pallas_call | solution.py:587
  180.0 6.3 %all-to-all-start = ((f32[8,32,384]{2,1,0:T(8,128)}), f32[8,32,384]{2,1,0:T(8,128)S(1)}, u32[]{:S(2)}, u32[]{:S(2)}) async-start(f32[8,32,384]{2,1,0:T(8,128)} %select_reduce_fusion), calls=%async_computation | async-start | bytes 786432 | tf_op jit(solution)/shard_map/all_to_all | solution.py:855
  187.0 5.7 %input_grad.1 = bf16[16,128,384]{2,1,0:T(8,128)(2,1)} custom-call(s32[34]{0:T(128)} %pad_add_fusion.refs_0_, bf16[16,128,384]{2,1,0:T(8,128)(2,1)} %refs_4_.14, bf16[16,128,384]{2,1,0:T(8,128)(2,1)} %refs_4_.14, bf16[16,128,384]{2,1,0:T(8,128)(2,1)} %refs_4_.14, bf16[16,128,384]{2,1,0:T(8,128)(2,1)} %refs_4_.14, f32[16,128,128]{2,1,0:T(8,128)} %get-tuple-element.74.refs_5_, ...), custom_call_target="tpu_custom_call" | custom-call | bytes 12910592 | tf_op jit(solution)/shard_map/input_grad/pallas_call | solution.py:587
  194.4 4.8 %w_grad.13 = bf16[384,1536]{1,0:T(8,128)(2,1)} custom-call(s32[34]{0:T(128)} %pad_add_fusion.refs_0_, s32[32]{0:T(128)} %pad_add_fusion.1.refs_1_, bf16[4,384,512]{2,1,0:T(8,128)(2,1)} %get-tuple-element.60.refs_2_, bf16[4,384,512]{2,1,0:T(8,128)(2,1)} %collective-permute-done.13.refs_3_, bf16[16,128,384]{2,1,0:T(8,128)(2,1)} %refs_4_.14, ...), custom_call_target="tpu_custom_call" | custom-call | flops 36238786560 | bytes 542638080 | tf_op jit(solution)/shard_map/w_grad/pallas_call | solution.py:587
  (138 shorter events, 31.7 us)
Async XLA Ops:
  2.1 5.0 %collective-permute-start = (bf16[1,48,384]{2,1,0:T(8,128)(2,1)S(1)}, bf16[1,48,384]{2,1,0:T(8,128)(2,1)S(1)}, u32[]{:S(2)}, u32[]{:S(2)}) collective-permute-start(bf16[1,48,384]{2,1,0:T(8,128)(2,1)S(1)} %fusion.5), channel_id=1, source_target_pairs={{0,4},{4,0},{8,12},{12,8},{16,20},{20,16},{24,28},{28,24},{1,5},{5... | collective-permute-start | bytes 110600 | tf_op jit(solution)/shard_map/ppermute | solution.py:562
  7.1 6.5 %collective-permute-start.1 = (bf16[2,48,384]{2,1,0:T(8,128)(2,1)S(1)}, bf16[2,48,384]{2,1,0:T(8,128)(2,1)S(1)}, u32[]{:S(2)}, u32[]{:S(2)}) collective-permute-start(bf16[2,48,384]{2,1,0:T(8,128)(2,1)S(1)} %pad_maximum_fusion.1.refs_0_), channel_id=1, source_target_pairs={{0,8},{4,12},{8,0},{12,4},{16,24},{20,28},{24,16},{28,20},{1,9},{5... | collective-permute-start | bytes 221192 | tf_op jit(solution)/shard_map/ppermute | solution.py:616
  9.2 6.8 %collective-permute-start.2 = (bf16[2,48,384]{2,1,0:T(8,128)(2,1)S(1)}, bf16[2,48,384]{2,1,0:T(8,128)(2,1)S(1)}, u32[]{:S(2)}, u32[]{:S(2)}) collective-permute-start(bf16[2,48,384]{2,1,0:T(8,128)(2,1)S(1)} %pad_maximum_fusion.1.refs_0_), channel_id=1, source_target_pairs={{0,16},{4,20},{8,24},{12,28},{16,0},{20,4},{24,8},{28,12},{1,17},{... | collective-permute-start | bytes 221192 | tf_op jit(solution)/shard_map/ppermute | solution.py:616
  11.8 6.2 %collective-permute-start.3 = (bf16[2,48,384]{2,1,0:T(8,128)(2,1)S(1)}, bf16[2,48,384]{2,1,0:T(8,128)(2,1)S(1)}, u32[]{:S(2)}, u32[]{:S(2)}) collective-permute-start(bf16[2,48,384]{2,1,0:T(8,128)(2,1)S(1)} %pad_maximum_fusion.1.refs_0_), channel_id=1, source_target_pairs={{0,24},{4,28},{8,16},{12,20},{16,8},{20,12},{24,0},{28,4},{1,25},{... | collective-permute-start | bytes 221192 | tf_op jit(solution)/shard_map/ppermute | solution.py:616
  18.0 27.3 %collective-permute-start.7 = (bf16[1536,384]{1,0:T(8,128)(2,1)S(1)}, bf16[1536,384]{1,0:T(8,128)(2,1)}, u32[]{:S(2)}, u32[]{:S(2)}) collective-permute-start(bf16[1536,384]{1,0:T(8,128)(2,1)S(1)} %bitcast.16), channel_id=1, source_target_pairs={{0,8},{4,12},{8,16},{12,20},{16,24},{20,28},{24,0},{28,4},{1,9},{5... | collective-permute-start | bytes 3538952 | tf_op jit(solution)/shard_map/ppermute | solution.py:565
  22.8 4.3 %collective-permute-start.4 = (f32[16,8,128]{2,1,0:T(8,128)}, f32[16,8,128]{2,1,0:T(8,128)S(1)}, u32[]{:S(2)}, u32[]{:S(2)}) collective-permute-start(f32[16,8,128]{2,1,0:T(8,128)} %frame_stats.1.refs_5_.refs_6_.refs_7_.refs_8_), channel_id=1, source_target_pairs={{0,1},{1,0},{2,3},{3,2},{4,5},{5,4},{6,7},{7,6},{8,9},{9,8},{10,11... | collective-permute-start | bytes 196616 | tf_op jit(solution)/shard_map/ppermute | solution.py:568
  22.8 4.8 %collective-permute-start.5 = (f32[16,8,128]{2,1,0:T(8,128)}, f32[16,8,128]{2,1,0:T(8,128)S(1)}, u32[]{:S(2)}, u32[]{:S(2)}) collective-permute-start(f32[16,8,128]{2,1,0:T(8,128)} %frame_stats.1.refs_5_.refs_6_.refs_7_.refs_8_), channel_id=1, source_target_pairs={{0,2},{1,3},{2,0},{3,1},{4,6},{5,7},{6,4},{7,5},{8,10},{9,11},{10,... | collective-permute-start | bytes 196616 | tf_op jit(solution)/shard_map/ppermute | solution.py:568
  24.3 4.3 %collective-permute-start.6 = (f32[16,8,128]{2,1,0:T(8,128)}, f32[16,8,128]{2,1,0:T(8,128)S(1)}, u32[]{:S(2)}, u32[]{:S(2)}) collective-permute-start(f32[16,8,128]{2,1,0:T(8,128)} %frame_stats.1.refs_5_.refs_6_.refs_7_.refs_8_), channel_id=1, source_target_pairs={{0,3},{1,2},{2,1},{3,0},{4,7},{5,6},{6,5},{7,4},{8,11},{9,10},{10,... | collective-permute-start | bytes 196616 | tf_op jit(solution)/shard_map/ppermute | solution.py:568
  25.5 36.7 %collective-permute-start.10 = (bf16[16,128,384]{2,1,0:T(8,128)(2,1)S(1)}, bf16[16,128,384]{2,1,0:T(8,128)(2,1)}, u32[]{:S(2)}, u32[]{:S(2)}) collective-permute-start(bf16[16,128,384]{2,1,0:T(8,128)(2,1)S(1)} %copy-done), channel_id=1, source_target_pairs={{0,4},{4,0},{8,12},{12,8},{16,20},{20,16},{24,28},{28,24},{1,5},{5... | collective-permute-start | bytes 4718600 | tf_op jit(solution)/shard_map/ppermute | solution.py:562
  28.6 36.9 %collective-permute-start.11 = (bf16[16,128,384]{2,1,0:T(8,128)(2,1)S(1)}, bf16[16,128,384]{2,1,0:T(8,128)(2,1)}, u32[]{:S(2)}, u32[]{:S(2)}) collective-permute-start(bf16[16,128,384]{2,1,0:T(8,128)(2,1)S(1)} %copy-done), channel_id=1, source_target_pairs={{0,2},{1,3},{2,0},{3,1},{4,6},{5,7},{6,4},{7,5},{8,10},{9,11},{10,... | collective-permute-start | bytes 4718600 | tf_op jit(solution)/shard_map/ppermute | solution.py:568
  33.1 32.5 %collective-permute-start.12 = (bf16[16,128,384]{2,1,0:T(8,128)(2,1)S(1)}, bf16[16,128,384]{2,1,0:T(8,128)(2,1)}, u32[]{:S(2)}, u32[]{:S(2)}) collective-permute-start(bf16[16,128,384]{2,1,0:T(8,128)(2,1)S(1)} %copy-done), channel_id=1, source_target_pairs={{0,1},{1,0},{2,3},{3,2},{4,5},{5,4},{6,7},{7,6},{8,9},{9,8},{10,11... | collective-permute-start | bytes 4718600 | tf_op jit(solution)/shard_map/ppermute | solution.py:568
  45.3 26.5 %collective-permute-start.8 = (bf16[1536,384]{1,0:T(8,128)(2,1)}, bf16[1536,384]{1,0:T(8,128)(2,1)S(1)}, u32[]{:S(2)}, u32[]{:S(2)}) collective-permute-start(bf16[1536,384]{1,0:T(8,128)(2,1)} %collective-permute-done.7.refs_7_), channel_id=1, source_target_pairs={{0,8},{4,12},{8,16},{12,20},{16,24},{20,28},{24,0},{28,4},{1,9},{5... | collective-permute-start | bytes 3538952 | tf_op jit(solution)/shard_map/ppermute | solution.py:565
  65.5 7.4 %collective-permute-start.14 = (bf16[16,128,384]{2,1,0:T(8,128)(2,1)}, bf16[16,128,384]{2,1,0:T(8,128)(2,1)}, u32[]{:S(2)}, u32[]{:S(2)}) collective-permute-start(bf16[16,128,384]{2,1,0:T(8,128)(2,1)} %collective-permute-done.10.refs_6_.refs_2_.refs_8_), channel_id=1, source_target_pairs={{0,1},{1,0},{2,3},{3,2},{4,5},{5,4},{6,7},{7,6},{8,9},{9,8},{10,11... | collective-permute-start | bytes 4718600 | tf_op jit(solution)/shard_map/ppermute | solution.py:568
  65.5 37.1 %collective-permute-start.16 = (bf16[16,128,384]{2,1,0:T(8,128)(2,1)}, bf16[16,128,384]{2,1,0:T(8,128)(2,1)}, u32[]{:S(2)}, u32[]{:S(2)}) collective-permute-start(bf16[16,128,384]{2,1,0:T(8,128)(2,1)} %collective-permute-done.10.refs_6_.refs_2_.refs_8_), channel_id=1, source_target_pairs={{0,2},{1,3},{2,0},{3,1},{4,6},{5,7},{6,4},{7,5},{8,10},{9,11},{10,... | collective-permute-start | bytes 4718600 | tf_op jit(solution)/shard_map/ppermute | solution.py:568
  67.0 36.8 %collective-permute-start.13 = (bf16[4,384,512]{2,1,0:T(8,128)(2,1)}, bf16[4,384,512]{2,1,0:T(8,128)(2,1)}, u32[]{:S(2)}, u32[]{:S(2)}) collective-permute-start(bf16[4,384,512]{2,1,0:T(8,128)(2,1)} %get-tuple-element.60.refs_2_), channel_id=1, source_target_pairs={{0,4},{4,0},{8,12},{12,8},{16,20},{20,16},{24,28},{28,24},{1,5},{5... | collective-permute-start | bytes 4718600 | tf_op jit(solution)/shard_map/ppermute | solution.py:562
  71.8 35.6 %copy-start.2 = (bf16[1536,384]{1,0:T(8,128)(2,1)}, bf16[1536,384]{1,0:T(8,128)(2,1)S(1)}, u32[]{:S(2)}) copy-start(bf16[1536,384]{1,0:T(8,128)(2,1)S(1)} %collective-permute-done.8.refs_8_) | copy-start | bytes 3538948
  71.8 30.8 %collective-permute-start.9 = (bf16[1536,384]{1,0:T(8,128)(2,1)S(1)}, bf16[1536,384]{1,0:T(8,128)(2,1)S(1)}, u32[]{:S(2)}, u32[]{:S(2)}) collective-permute-start(bf16[1536,384]{1,0:T(8,128)(2,1)S(1)} %collective-permute-done.8.refs_8_), channel_id=1, source_target_pairs={{0,8},{4,12},{8,16},{12,20},{16,24},{20,28},{24,0},{28,4},{1,9},{5... | collective-permute-start | bytes 3538952 | tf_op jit(solution)/shard_map/ppermute | solution.py:565
  73.0 37.0 %collective-permute-start.15 = (bf16[16,128,384]{2,1,0:T(8,128)(2,1)}, bf16[16,128,384]{2,1,0:T(8,128)(2,1)}, u32[]{:S(2)}, u32[]{:S(2)}) collective-permute-start(bf16[16,128,384]{2,1,0:T(8,128)(2,1)} %collective-permute-done.11.refs_4_.refs_6_), channel_id=1, source_target_pairs={{0,1},{1,0},{2,3},{3,2},{4,5},{5,4},{6,7},{7,6},{8,9},{9,8},{10,11... | collective-permute-start | bytes 4718600 | tf_op jit(solution)/shard_map/ppermute | solution.py:568
  102.7 7.3 %collective-permute-start.17 = (bf16[16,128,384]{2,1,0:T(8,128)(2,1)}, bf16[16,128,384]{2,1,0:T(8,128)(2,1)}, u32[]{:S(2)}, u32[]{:S(2)}) collective-permute-start(bf16[16,128,384]{2,1,0:T(8,128)(2,1)} %collective-permute-done.16.refs_6_.refs_4_.refs_10_), channel_id=1, source_target_pairs={{0,1},{1,0},{2,3},{3,2},{4,5},{5,4},{6,7},{7,6},{8,9},{9,8},{10,11... | collective-permute-start | bytes 4718600 | tf_op jit(solution)/shard_map/ppermute | solution.py:568
  107.4 16.7 %collective-permute-start.18 = (bf16[384,768]{1,0:T(8,128)(2,1)}, bf16[384,768]{1,0:T(8,128)(2,1)S(1)}, u32[]{:S(2)}, u32[]{:S(2)}) collective-permute-start(bf16[384,768]{1,0:T(8,128)(2,1)} %w_grad.7), channel_id=1, source_target_pairs={{0,8},{4,12},{8,16},{12,20},{16,24},{20,28},{24,0},{28,4},{1,9},{5... | collective-permute-start | bytes 1769480 | tf_op jit(solution)/shard_map/ppermute | solution.py:565
  120.9 14.8 %collective-permute-start.20 = (bf16[4,512,128]{2,1,0:T(8,128)(2,1)}, bf16[4,512,128]{2,1,0:T(8,128)(2,1)S(1)}, u32[]{:S(2)}, u32[]{:S(2)}) collective-permute-start(bf16[4,512,128]{2,1,0:T(8,128)(2,1)} %get-tuple-element.65), channel_id=1, source_target_pairs={{0,4},{4,0},{8,12},{12,8},{16,20},{20,16},{24,28},{28,24},{1,5},{5... | collective-permute-start | bytes 1572872 | tf_op jit(solution)/shard_map/ppermute | solution.py:562
  122.5 18.1 %collective-permute-start.19 = (bf16[384,768]{1,0:T(8,128)(2,1)S(1)}, bf16[384,768]{1,0:T(8,128)(2,1)S(1)}, u32[]{:S(2)}, u32[]{:S(2)}) collective-permute-start(bf16[384,768]{1,0:T(8,128)(2,1)S(1)} %copy-done.26), channel_id=1, source_target_pairs={{0,8},{4,12},{8,16},{12,20},{16,24},{20,28},{24,0},{28,4},{1,9},{5... | collective-permute-start | bytes 1769480 | tf_op jit(solution)/shard_map/ppermute | solution.py:565
  128.7 30.9 %collective-permute-start.22 = (bf16[384,768]{1,0:T(8,128)(2,1)}, bf16[384,768]{1,0:T(8,128)(2,1)S(1)}, u32[]{:S(2)}, u32[]{:S(2)}) collective-permute-start(bf16[384,768]{1,0:T(8,128)(2,1)} %w_grad.9), channel_id=1, source_target_pairs={{0,8},{4,12},{8,16},{12,20},{16,24},{20,28},{24,0},{28,4},{1,9},{5... | collective-permute-start | bytes 1769480 | tf_op jit(solution)/shard_map/ppermute | solution.py:565
  135.8 16.3 %collective-permute-start.21 = (bf16[4,512,128]{2,1,0:T(8,128)(2,1)S(1)}, bf16[4,512,128]{2,1,0:T(8,128)(2,1)S(1)}, u32[]{:S(2)}, u32[]{:S(2)}) collective-permute-start(bf16[4,512,128]{2,1,0:T(8,128)(2,1)S(1)} %copy-done.30), channel_id=1, source_target_pairs={{0,4},{4,0},{8,12},{12,8},{16,20},{20,16},{24,28},{28,24},{1,5},{5... | collective-permute-start | bytes 1572872 | tf_op jit(solution)/shard_map/ppermute | solution.py:562
  145.1 26.7 %collective-permute-start.24 = (bf16[384,768]{1,0:T(8,128)(2,1)}, bf16[384,768]{1,0:T(8,128)(2,1)S(1)}, u32[]{:S(2)}, u32[]{:S(2)}) collective-permute-start(bf16[384,768]{1,0:T(8,128)(2,1)} %w_grad.10), channel_id=1, source_target_pairs={{0,8},{4,12},{8,16},{12,20},{16,24},{20,28},{24,0},{28,4},{1,9},{5... | collective-permute-start | bytes 1769480 | tf_op jit(solution)/shard_map/ppermute | solution.py:565
  152.1 12.1 %collective-permute-start.23 = (bf16[4,512,128]{2,1,0:T(8,128)(2,1)S(1)}, bf16[4,512,128]{2,1,0:T(8,128)(2,1)S(1)}, u32[]{:S(2)}, u32[]{:S(2)}) collective-permute-start(bf16[4,512,128]{2,1,0:T(8,128)(2,1)S(1)} %copy-done.29), channel_id=1, source_target_pairs={{0,4},{4,0},{8,12},{12,8},{16,20},{20,16},{24,28},{28,24},{1,5},{5... | collective-permute-start | bytes 1572872 | tf_op jit(solution)/shard_map/ppermute | solution.py:562
  164.1 28.6 %collective-permute-start.28 = (bf16[384,768]{1,0:T(8,128)(2,1)}, bf16[384,768]{1,0:T(8,128)(2,1)S(1)}, u32[]{:S(2)}, u32[]{:S(2)}) collective-permute-start(bf16[384,768]{1,0:T(8,128)(2,1)} %w_grad.11), channel_id=1, source_target_pairs={{0,8},{4,12},{8,16},{12,20},{16,24},{20,28},{24,0},{28,4},{1,9},{5... | collective-permute-start | bytes 1769480 | tf_op jit(solution)/shard_map/ppermute | solution.py:565
  176.3 16.4 %collective-permute-start.29 = (bf16[384,768]{1,0:T(8,128)(2,1)}, bf16[384,768]{1,0:T(8,128)(2,1)S(1)}, u32[]{:S(2)}, u32[]{:S(2)}) collective-permute-start(bf16[384,768]{1,0:T(8,128)(2,1)} %w_grad.12), channel_id=1, source_target_pairs={{0,8},{4,12},{8,16},{12,20},{16,24},{20,28},{24,0},{28,4},{1,9},{5... | collective-permute-start | bytes 1769480 | tf_op jit(solution)/shard_map/ppermute | solution.py:565
  177.1 9.3 %collective-permute-start.25 = (f32[16,8,128]{2,1,0:T(8,128)S(1)}, f32[16,8,128]{2,1,0:T(8,128)S(1)}, u32[]{:S(2)}, u32[]{:S(2)}) collective-permute-start(f32[16,8,128]{2,1,0:T(8,128)S(1)} %add_add_fusion.refs_10_), channel_id=1, source_target_pairs={{0,1},{1,0},{2,3},{3,2},{4,5},{5,4},{6,7},{7,6},{8,9},{9,8},{10,11... | collective-permute-start | bytes 196616 | tf_op jit(solution)/shard_map/ppermute | solution.py:568
  177.1 9.2 %collective-permute-start.26 = (f32[16,8,128]{2,1,0:T(8,128)S(1)}, f32[16,8,128]{2,1,0:T(8,128)S(1)}, u32[]{:S(2)}, u32[]{:S(2)}) collective-permute-start(f32[16,8,128]{2,1,0:T(8,128)S(1)} %add_add_fusion.refs_10_), channel_id=1, source_target_pairs={{0,2},{1,3},{2,0},{3,1},{4,6},{5,7},{6,4},{7,5},{8,10},{9,11},{10,... | collective-permute-start | bytes 196616 | tf_op jit(solution)/shard_map/ppermute | solution.py:568
  178.5 7.8 %collective-permute-start.27 = (f32[16,8,128]{2,1,0:T(8,128)S(1)}, f32[16,8,128]{2,1,0:T(8,128)S(1)}, u32[]{:S(2)}, u32[]{:S(2)}) collective-permute-start(f32[16,8,128]{2,1,0:T(8,128)S(1)} %add_add_fusion.refs_10_), channel_id=1, source_target_pairs={{0,3},{1,2},{2,1},{3,0},{4,7},{5,6},{6,5},{7,4},{8,11},{9,10},{10,... | collective-permute-start | bytes 196616 | tf_op jit(solution)/shard_map/ppermute | solution.py:568
  180.0 19.2 %all-to-all-start = ((f32[8,32,384]{2,1,0:T(8,128)}), f32[8,32,384]{2,1,0:T(8,128)S(1)}, u32[]{:S(2)}, u32[]{:S(2)}) async-start(f32[8,32,384]{2,1,0:T(8,128)} %select_reduce_fusion), calls=%async_computation | async-start | bytes 786432 | tf_op jit(solution)/shard_map/all_to_all | solution.py:855
  (33 other events, 258.8 us)
